TPU v7x, 32 devices: a whole 2x2x4 slice. The times are simulated.
32 devices in a mesh: ctx: 16 (over z, y, core), ch: 2 (over x).
Axes of the slice: x: 2, y: 2, z: 4, core: 2. Of those that a mesh axis runs over, the one named last changes fastest.
Arguments:
- mamba_input: bfloat16 [1024, 16384], P(('ctx', 'ch')), may hold values from -6 to 6
- mamba_gate: bfloat16 [1024, 16384], P(('ctx', 'ch')), may hold values from -6 to 6
- conv_weight: float32 [4, 16384], P(None, 'ch'), may hold values from -3 to 3
- conv_bias: float32 [16384], P('ch'), may hold values from -3 to 3
- step_down: bfloat16 [16384, 512], P('ch'), may hold values from -0.046875 to 0.046875
- state_proj: bfloat16 [16384, 32], P('ch'), may hold values from -0.046875 to 0.046875
- step_up: bfloat16 [512, 16384], P(None, 'ch'), may hold values from -0.0625 to 0.0625
- step_bias: float32 [16384], P('ch'), may hold values from -5 to -4
- decay_rate: float32 [16, 16384], P(None, 'ch'), may hold values from 0 to 3, as said below
- skip_gain: float32 [16384], P('ch'), may hold values from 0.5 to 1.5
- queries: bfloat16 [1024, 8192], P('ctx', 'ch'), may hold values from -6 to 6
- key_rows: bfloat16 [1024, 1024], P('ctx', 'ch'), may hold values from -6 to 6
- value_rows: bfloat16 [1024, 1024], P('ctx', 'ch'), may hold values from -6 to 6
Outputs:
- mamba_out: bfloat16 [1024, 16384], P(('ctx', 'ch'))
- attention_out: bfloat16 [1024, 8192], P('ctx', 'ch')
Inputs may be any that keep to these rules, and one draw needn't show every extreme that they name: `decay_rate`: positive decay rates.
All inputs are finite; a program needn't handle non-finite values.
Results may differ from a plain program's by a relative error of at most 0.013.
Values may be sent and summed in bfloat16 or wider, within the bound.
A program may use at most 320 MiB of HBM per device.

v0:
```python
import math

import jax
import jax.numpy as jnp
from jax import lax
from jax.sharding import PartitionSpec as P

STATE = 16
CONV = 4
HEADS = 64
KV_HEADS = 8
HEAD_DIM = 128


def passed_along(array, axis, by):
    size = lax.axis_size(axis)
    pairs = [(i, i + by) for i in range(size) if 0 <= i + by < size]
    return lax.ppermute(array, axis, pairs)


def scan_pair(earlier, later):
    return (earlier[0] * later[0], later[0] * earlier[1] + later[1])


def local_scan(step_size, activation_f, state_terms, decay_rate):
    rows_here, channels = step_size.shape
    block_len = math.gcd(rows_here, 32)

    def local_one_block(block_index, loop_state):
        carried, running, outputs, totals = loop_state
        first_row = block_index * block_len
        step_block = lax.dynamic_slice_in_dim(step_size, first_row, block_len, 0)
        act_block = lax.dynamic_slice_in_dim(activation_f, first_row, block_len, 0)
        term_block = lax.dynamic_slice_in_dim(state_terms, first_row, block_len, 0)
        input_mix = term_block[:, :STATE]
        output_mix = term_block[:, STATE:]
        decays = jnp.exp(-decay_rate[None, :, :] * step_block[:, None, :])
        pushes = (step_block * act_block)[:, None, :] * input_mix[:, :, None]
        joint_decay, joint_push = lax.associative_scan(scan_pair, (decays, pushes), axis=0)
        states = joint_push + joint_decay * carried[None, :, :]
        block_out = jnp.sum(output_mix[:, :, None] * states, axis=1)
        cumulative = running[None, :] + jnp.cumsum(step_block, axis=0)
        outputs = lax.dynamic_update_slice_in_dim(outputs, block_out, first_row, 0)
        totals = lax.dynamic_update_slice_in_dim(totals, cumulative, first_row, 0)
        return (states[-1], cumulative[-1], outputs, totals)

    initial = (
        jnp.zeros((STATE, channels), jnp.float32),
        jnp.zeros((channels,), jnp.float32),
        jnp.zeros((rows_here, channels), jnp.float32),
        jnp.zeros((rows_here, channels), jnp.float32),
    )
    return lax.fori_loop(0, rows_here // block_len, local_one_block, initial)


def add_incoming(outputs, totals, state_terms, decay_rate, incoming):
    rows_here = outputs.shape[0]
    block_len = math.gcd(rows_here, 32)

    def add_one_block(block_index, current):
        first_row = block_index * block_len
        total_block = lax.dynamic_slice_in_dim(totals, first_row, block_len, 0)
        output_mix = lax.dynamic_slice_in_dim(state_terms, first_row, block_len, 0)[:, STATE:]
        carried_in = (
            jnp.exp(-decay_rate[None, :, :] * total_block[:, None, :]) * incoming[None, :, :]
        )
        extra = jnp.sum(output_mix[:, :, None] * carried_in, axis=1)
        old_block = lax.dynamic_slice_in_dim(current, first_row, block_len, 0)
        return lax.dynamic_update_slice_in_dim(current, old_block + extra, first_row, 0)

    return lax.fori_loop(0, rows_here // block_len, add_one_block, outputs)


def attend(queries, key_rows, value_rows):
    rows_here = queries.shape[0]
    groups_here = key_rows.shape[1] // HEAD_DIM
    group_size = HEADS // KV_HEADS
    scale_factor = 1.0 / math.sqrt(HEAD_DIM)
    query_heads = queries.reshape(rows_here, groups_here, group_size, HEAD_DIM)
    query_first = lax.axis_index("ctx") * rows_here
    query_pos = query_first + jnp.arange(rows_here, dtype=jnp.int32)
    initial = (
        jnp.full((groups_here, group_size, rows_here), -1e30, jnp.float32),
        jnp.zeros((groups_here, group_size, rows_here), jnp.float32),
        jnp.zeros((groups_here, group_size, rows_here, HEAD_DIM), jnp.float32),
    )
    key_piece = lax.all_gather(key_rows, "ctx", axis=0, tiled=True)
    value_piece = lax.all_gather(value_rows, "ctx", axis=0, tiled=True)
    piece_rows = key_piece.shape[0]
    block_len = math.gcd(piece_rows, 512)

    def fold_one_block(block_index, inner_state):
        block_first = block_index * block_len
        key_block = lax.dynamic_slice_in_dim(
            key_piece, block_index * block_len, block_len, 0
        ).reshape(block_len, groups_here, HEAD_DIM)
        value_block = lax.dynamic_slice_in_dim(
            value_piece, block_index * block_len, block_len, 0
        ).reshape(block_len, groups_here, HEAD_DIM)

        def visit(visit_state):
            running_max, running_total, running_sum = visit_state
            scores = (
                jnp.einsum(
                    "tkgd,skd->kgts", query_heads, key_block, preferred_element_type=jnp.float32
                )
                * scale_factor
            )
            visible = (block_first + jnp.arange(block_len, dtype=jnp.int32))[None, :] <= query_pos[
                :, None
            ]
            masked = jnp.where(visible, scores, -1e30)
            new_max = jnp.maximum(running_max, jnp.max(masked, axis=3))
            weights = jnp.where(visible, jnp.exp(masked - new_max[..., None]), 0.0)
            rescale = jnp.exp(running_max - new_max)
            new_total = running_total * rescale + jnp.sum(weights, axis=3)
            new_sum = running_sum * rescale[..., None] + jnp.einsum(
                "kgts,skd->kgtd",
                weights.astype(jnp.bfloat16),
                value_block,
                preferred_element_type=jnp.float32,
            )
            return (new_max, new_total, new_sum)

        return lax.cond(
            block_first > query_first + rows_here - 1, lambda skipped: skipped, visit, inner_state
        )

    final_max, final_total, final_sum = lax.fori_loop(
        0, piece_rows // block_len, fold_one_block, initial
    )
    mixed = final_sum / final_total[..., None]
    return (
        mixed.transpose(2, 0, 1, 3)
        .reshape(rows_here, groups_here * group_size * HEAD_DIM)
        .astype(jnp.bfloat16)
    )


def local(
    mamba_input,
    mamba_gate,
    conv_weight,
    conv_bias,
    step_down,
    state_proj,
    step_up,
    step_bias,
    decay_rate,
    skip_gain,
    queries,
    key_rows,
    value_rows,
):
    inner_in, inner_gate = (
        lax.all_to_all(mamba_input, "ch", split_axis=1, concat_axis=0, tiled=True),
        lax.all_to_all(mamba_gate, "ch", split_axis=1, concat_axis=0, tiled=True),
    )
    rows_here = inner_in.shape[0]
    rim_rows = passed_along(inner_in[rows_here - (CONV - 1) :], "ctx", 1)
    padded = jnp.concatenate([rim_rows, inner_in], axis=0).astype(jnp.float32)
    conv_sum = conv_bias[None, :] + sum(
        (
            conv_weight[tap_index][None, :] * padded[tap_index : tap_index + rows_here]
            for tap_index in range(CONV)
        )
    )
    activation = jax.nn.silu(conv_sum).astype(jnp.bfloat16)
    low_part = jnp.dot(activation, step_down, preferred_element_type=jnp.float32)
    term_part = jnp.dot(activation, state_proj, preferred_element_type=jnp.float32)
    step_low, state_terms = (
        lax.psum(low_part.astype(jnp.bfloat16), "ch").astype(jnp.float32),
        lax.psum(term_part.astype(jnp.bfloat16), "ch").astype(jnp.float32),
    )
    step_size = jax.nn.softplus(
        jnp.dot(step_low.astype(jnp.bfloat16), step_up, preferred_element_type=jnp.float32)
        + step_bias[None, :]
    )
    activation_f = activation.astype(jnp.float32)
    end_state, running_end, outputs, totals = local_scan(
        step_size, activation_f, state_terms, decay_rate
    )
    whole_decay = jnp.exp(-decay_rate * running_end[None, :])

    def relay_step(step_index, incoming):
        return passed_along(whole_decay * incoming + end_state, "ctx", 1)

    incoming = lax.fori_loop(0, lax.axis_size("ctx") - 1, relay_step, jnp.zeros_like(end_state))
    outputs = add_incoming(outputs, totals, state_terms, decay_rate, incoming)
    scan_out = (outputs + skip_gain[None, :] * activation_f).astype(jnp.bfloat16)
    scan_out = lax.optimization_barrier(scan_out)
    outgoing = (scan_out.astype(jnp.float32) * jax.nn.silu(inner_gate.astype(jnp.float32))).astype(
        jnp.bfloat16
    )
    mamba_out = lax.all_to_all(outgoing, "ch", split_axis=0, concat_axis=1, tiled=True)
    attention_out = attend(queries, key_rows, value_rows)
    return (mamba_out, attention_out)


def solution(mesh):
    placed = (
        P(("ctx", "ch"), None),
        P(("ctx", "ch"), None),
        P(None, "ch"),
        P("ch"),
        P("ch", None),
        P("ch", None),
        P(None, "ch"),
        P("ch"),
        P(None, "ch"),
        P("ch"),
        P("ctx", "ch"),
        P("ctx", "ch"),
        P("ctx", "ch"),
    )
    return jax.shard_map(
        local,
        mesh=mesh,
        in_specs=placed,
        out_specs=(P(("ctx", "ch"), None), P("ctx", "ch")),
        check_vma=False,
    )
```

profile of v0, /device:TPU:16, one launch (start us, length us, event | category | flops | bytes accessed | tf_op | source)
XLA Modules:
  0.0 1040.9 jit_solution(4191055125861514580)
XLA Ops:
  9.4 16.3 %all_to_all.51 = bf16[32,2,8192]{2,0,1:T(8,128)(2,1)S(1)} all-to-all(bf16[32,2,8192]{2,0,1:T(8,128)(2,1)S(1)} %bitcast.100), channel_id=1, replica_groups=mesh['ctx'=16,'ch'=2] {'ch'}, dimensions={1} | all-to-all | bytes 2097152 | tf_op jit(solution)/shard_map/all_to_all | solution.py:156
  47.1 11.5 %psum.15 = bf16[64,32]{0,1:T(8,128)(2,1)S(1)} all-reduce(bf16[64,32]{0,1:T(8,128)(2,1)S(1)} %convolution_convert_fusion.1), channel_id=1, replica_groups=mesh['ctx'=16,'ch'=2] {'ch'}, use_global_device_ids=true, to_apply=%region_1.2 | all-reduce | flops 2048 | bytes 8192 | tf_op jit(solution)/shard_map/psum | solution.py:173
  71.1 703.1 %while.66 = (s32[]{:T(128)}, f32[16,8192]{1,0:T(8,128)}, f32[8192]{0:T(1024)}, f32[64,8192]{1,0:T(8,128)}, f32[64,8192]{1,0:T(8,128)}, /*index=5*/f32[64,8192]{1...) while((s32[]{:T(128)}, f32[16,8192]{1,0:T(8,128)}, ...), condition=%wide.region_5.6_spmd, body=%wide.region_2.5_spmd.sunk | while | flops 86900744 | bytes 752144896 | solution.py:53
  90.7 18.3 %slice_add_fusion.10 = (f32[16,16,8192]{2,1,0:T(8,128)}, f32[16,16,8192]{2,1,0:T(8,128)}) fusion(f32[32,16,8192]{2,1,0:T(8,128)} %broadcast_multiply_fusion.2, f32[32,16,8192]{2,1,0:T(8,128)} %multiply_exponential_fusion.3), kind=kLoop, calls=%fused_computation.7.clone.1 | loop fusion | flops 6291456 | bytes 50331648 | tf_op jit(solution)/shard_map/while/body/eval_jaxpr/add | solution.py:22
  173.3 10.0 pad.304
  212.2 9.9 pad.307
  228.1 9.9 pad.308
  243.6 9.8 pad.309
  253.4 22.9 %fusion.51 = (f32[15,16,8192]{2,1,0:T(8,128)}, f32[15,16,8192]{2,1,0:T(8,128)}) fusion(f32[16,16,8192]{2,1,0:T(8,128)} %pad.304, f32[16,16,8192]{2,1,0:T(8,128)} %pad.307, f32[32,16,8192]{2,1,0:T(8,128)} %broadcast_multiply_fusion.2, f32[32,16,8192]{2,1,0:T(8,128)} %multiply_exponential_fusion.3, f32[16,16,8192]{2,1,0:T(8,128)} %pad.308, ...), kind=kLoop, calls=%fused_computation.11.clone.1 | loop fusion | flops 9830400 | bytes 62914560 | tf_op jit(solution)/shard_map/while/body/eval_jaxpr/add | solution.py:22
  283.7 17.6 %pad.310 = f32[32,16,8192]{2,1,0:T(8,128)} pad(f32[16,16,8192]{2,1,0:T(8,128)} %pad_maximum_fusion.22, f32[]{:T(128)} %constant.194.clone.1..sunk), padding=0_1_1x0_0_0x0_0_0 | pad | bytes 25165828 | tf_op jit(solution)/shard_map/while/body/eval_jaxpr/pad | solution.py:39
  301.3 10.3 add.614
  311.6 17.6 %pad.311 = f32[32,16,8192]{2,1,0:T(8,128)} pad(f32[16,16,8192]{2,1,0:T(8,128)} %add.614, f32[]{:T(128)} %constant.194.clone.1..sunk), padding=1_0_1x0_0_0x0_0_0 | pad | bytes 25165828 | tf_op jit(solution)/shard_map/while/body/eval_jaxpr/pad | solution.py:39
  336.6 17.6 %pad.312 = f32[32,16,8192]{2,1,0:T(8,128)} pad(f32[16,16,8192]{2,1,0:T(8,128)} %pad_maximum_fusion.23, f32[]{:T(128)} %constant.194.clone.1..sunk), padding=0_1_1x0_0_0x0_0_0 | pad | bytes 25165828 | tf_op jit(solution)/shard_map/while/body/eval_jaxpr/pad | solution.py:39
  354.2 10.4 add.615
  364.5 17.6 %pad.313 = f32[32,16,8192]{2,1,0:T(8,128)} pad(f32[16,16,8192]{2,1,0:T(8,128)} %add.615, f32[]{:T(128)} %constant.194.clone.1..sunk), padding=1_0_1x0_0_0x0_0_0 | pad | bytes 25165828 | tf_op jit(solution)/shard_map/while/body/eval_jaxpr/pad | solution.py:39
  382.2 30.2 %multiply_reduce_fusion.4 = (f32[32,8192]{1,0:T(8,128)S(1)}, f32[32,16,8192]{2,1,0:T(8,128)}) fusion(f32[32,16]{1,0:T(8,128)S(1)} %copy-done.20, f32[16,8192]{1,0:T(8,128)S(1)} %copy-done.10, f32[32,16,8192]{2,1,0:T(8,128)} %pad.310, f32[32,16,8192]{2,1,0:T(8,128)} %pad.311, f32[32,16,8192]{2,1,0:T(8,128)} %pad.312, f32[32,16,8192]{2,1,0:T(8,128)} %pad.313), kind=kLoop, calls=%fused_computation.1.clone.1 | loop fusion | flops 24903680 | bytes 85460992 | tf_op jit(solution)/shard_map/while/body/eval_jaxpr/reduce_sum | solution.py:41
  438.9 18.2 %slice_add_fusion.10 = (f32[16,16,8192]{2,1,0:T(8,128)}, f32[16,16,8192]{2,1,0:T(8,128)}) fusion(f32[32,16,8192]{2,1,0:T(8,128)} %broadcast_multiply_fusion.2, f32[32,16,8192]{2,1,0:T(8,128)} %multiply_exponential_fusion.3), kind=kLoop, calls=%fused_computation.7.clone.1 | loop fusion | flops 6291456 | bytes 50331648 | tf_op jit(solution)/shard_map/while/body/eval_jaxpr/add | solution.py:22
  521.4 10.0 pad.304
  560.2 9.9 pad.307
  576.2 9.9 pad.308
  591.7 9.8 pad.309
  601.5 22.9 %fusion.51 = (f32[15,16,8192]{2,1,0:T(8,128)}, f32[15,16,8192]{2,1,0:T(8,128)}) fusion(f32[16,16,8192]{2,1,0:T(8,128)} %pad.304, f32[16,16,8192]{2,1,0:T(8,128)} %pad.307, f32[32,16,8192]{2,1,0:T(8,128)} %broadcast_multiply_fusion.2, f32[32,16,8192]{2,1,0:T(8,128)} %multiply_exponential_fusion.3, f32[16,16,8192]{2,1,0:T(8,128)} %pad.308, ...), kind=kLoop, calls=%fused_computation.11.clone.1 | loop fusion | flops 9830400 | bytes 62914560 | tf_op jit(solution)/shard_map/while/body/eval_jaxpr/add | solution.py:22
  631.7 17.6 %pad.310 = f32[32,16,8192]{2,1,0:T(8,128)} pad(f32[16,16,8192]{2,1,0:T(8,128)} %pad_maximum_fusion.22, f32[]{:T(128)} %constant.194.clone.1..sunk), padding=0_1_1x0_0_0x0_0_0 | pad | bytes 25165828 | tf_op jit(solution)/shard_map/while/body/eval_jaxpr/pad | solution.py:39
  649.4 10.3 add.614
  659.6 17.6 %pad.311 = f32[32,16,8192]{2,1,0:T(8,128)} pad(f32[16,16,8192]{2,1,0:T(8,128)} %add.614, f32[]{:T(128)} %constant.194.clone.1..sunk), padding=1_0_1x0_0_0x0_0_0 | pad | bytes 25165828 | tf_op jit(solution)/shard_map/while/body/eval_jaxpr/pad | solution.py:39
  684.6 17.6 %pad.312 = f32[32,16,8192]{2,1,0:T(8,128)} pad(f32[16,16,8192]{2,1,0:T(8,128)} %pad_maximum_fusion.23, f32[]{:T(128)} %constant.194.clone.1..sunk), padding=0_1_1x0_0_0x0_0_0 | pad | bytes 25165828 | tf_op jit(solution)/shard_map/while/body/eval_jaxpr/pad | solution.py:39
  702.2 10.4 add.615
  712.6 17.6 %pad.313 = f32[32,16,8192]{2,1,0:T(8,128)} pad(f32[16,16,8192]{2,1,0:T(8,128)} %add.615, f32[]{:T(128)} %constant.194.clone.1..sunk), padding=1_0_1x0_0_0x0_0_0 | pad | bytes 25165828 | tf_op jit(solution)/shard_map/while/body/eval_jaxpr/pad | solution.py:39
  730.2 30.2 %multiply_reduce_fusion.4 = (f32[32,8192]{1,0:T(8,128)S(1)}, f32[32,16,8192]{2,1,0:T(8,128)}) fusion(f32[32,16]{1,0:T(8,128)S(1)} %copy-done.20, f32[16,8192]{1,0:T(8,128)S(1)} %copy-done.10, f32[32,16,8192]{2,1,0:T(8,128)} %pad.310, f32[32,16,8192]{2,1,0:T(8,128)} %pad.311, f32[32,16,8192]{2,1,0:T(8,128)} %pad.312, f32[32,16,8192]{2,1,0:T(8,128)} %pad.313), kind=kLoop, calls=%fused_computation.1.clone.1 | loop fusion | flops 24903680 | bytes 85460992 | tf_op jit(solution)/shard_map/while/body/eval_jaxpr/reduce_sum | solution.py:41
  775.4 202.8 %while.67 = (s32[]{:T(128)}, f32[16,8192]{1,0:T(8,128)S(1)}, f32[16,8192]{1,0:T(8,128)S(1)}, f32[16,8192]{1,0:T(8,128)}, s32[]{:T(128)}) while((s32[]{:T(128)}, f32[16,8192]{1,0:T(8,128)S(1)}, f32[16,8192]{1,0:T(8,128)S(1)}, f32[16,8192]{1,0:T(8,128)}, s32[]{:T(128)}) %tuple.208), condition=%wide.region_7.8_spmd, body=%wide.region_6.7_spmd.sunk | while | flops 262146 | bytes 4194405 | solution.py:188
  978.2 18.2 %while.68 = (s32[]{:T(128)}, f32[64,8192]{1,0:T(8,128)S(1)}, f32[64,32]{1,0:T(8,128)S(1)}, f32[1,16,8192]{2,1,0:T(8,128)}, f32[64,8192]{1,0:T(8,128)}, /*index=5...) while((s32[]{:T(128)}, f32[64,8192]{1,0:T(8,128)S(1)}, ...), condition=%wide.region_10.11_spmd, body=%wide.region_8.10_spmd.sunk | while | flops 16777224 | bytes 8394939 | solution.py:71
  1020.3 10.1 while.69
  (303 shorter events, 595.6 us)
Async XLA Ops:
  8.0 38.7 %copy-start = (bf16[8192,32]{0,1:T(8,128)(2,1)S(1)}, bf16[8192,32]{0,1:T(8,128)(2,1)}, u32[]{:S(2)}) copy-start(bf16[8192,32]{0,1:T(8,128)(2,1)} %param.28) | copy-start | bytes 1572868
  8.0 24.6 %copy-start.25 = (f32[8192]{0:T(1024)S(1)}, f32[8192]{0:T(1024)}, u32[]{:S(2)}) copy-start(f32[8192]{0:T(1024)} %param.26) | copy-start | bytes 98308
  8.0 51.4 %all-reduce.22.cloned.1.call-start = ((), (), s32[]{:S(2)}) async-start(), calls=%async_computation.3 | async-start | bytes 131072 | tf_op jit(solution)/shard_map/psum | solution.py:172
  25.8 6.5 collective-permute-start.1
  39.2 20.3 %copy-start.26 = (f32[8192]{0:T(1024)S(1)}, f32[8192]{0:T(1024)}, u32[]{:S(2)}) copy-start(f32[8192]{0:T(1024)} %param.30) | copy-start | bytes 98308
  39.2 976.9 %all-gather.3.cloned.1.call-start = ((), (), s32[]{:S(2)}) async-start(), calls=%async_computation.4 | async-start | bytes 1114112 | tf_op jit(solution)/shard_map/all_gather | solution.py:87
  40.8 958.1 %all-to-all-start.1 = ((bf16[32,2,8192]{2,0,1:T(8,128)(2,1)}), bf16[32,2,8192]{2,0,1:T(8,128)(2,1)}, u32[]{:S(2)}, u32[]{:S(2)}) async-start(bf16[32,2,8192]{2,0,1:T(8,128)(2,1)} %bitcast.82), calls=%async_computation.1 | async-start | bytes 2097152 | tf_op jit(solution)/shard_map/all_to_all | solution.py:157
  45.2 972.4 %all-gather.5.cloned.1.call-start = ((), (), s32[]{:S(2)}) async-start(), calls=%async_computation.5 | async-start | bytes 1114112 | tf_op jit(solution)/shard_map/all_gather | solution.py:88
  253.4 22.9 %slice-start.1 = ((f32[32,16,8192]{2,1,0:T(8,128)}), f32[1,16,8192]{2,1,0:T(8,128)S(1)}, s32[]{:S(2)}) async-start(f32[32,16,8192]{2,1,0:T(8,128)} %multiply_exponential_fusion.3), calls=%async_computation.7 | async-start | bytes 1048576 | tf_op jit(solution)/shard_map/while/body/eval_jaxpr/slice | solution.py:39
  382.1 32.1 %copy-start.7 = (f32[32,8192]{1,0:T(8,128)S(1)}, f32[32,8192]{1,0:T(8,128)}, u32[]{:S(2)}) copy-start(f32[32,8192]{1,0:T(8,128)} %copy-done.6) | copy-start | bytes 3145732 | tf_op jit(solution)/shard_map/while
  382.2 34.0 %copy-start.21 = (f32[8192]{0:T(1024)S(1)}, f32[8192]{0:T(1024)}, u32[]{:S(2)}) copy-start(f32[8192]{0:T(1024)} %get-tuple-element.1232) | copy-start | bytes 98308 | tf_op jit(solution)/shard_map/while
  601.5 22.9 %slice-start.1 = ((f32[32,16,8192]{2,1,0:T(8,128)}), f32[1,16,8192]{2,1,0:T(8,128)S(1)}, s32[]{:S(2)}) async-start(f32[32,16,8192]{2,1,0:T(8,128)} %multiply_exponential_fusion.3), calls=%async_computation.7 | async-start | bytes 1048576 | tf_op jit(solution)/shard_map/while/body/eval_jaxpr/slice | solution.py:39
  730.2 32.1 %copy-start.7 = (f32[32,8192]{1,0:T(8,128)S(1)}, f32[32,8192]{1,0:T(8,128)}, u32[]{:S(2)}) copy-start(f32[32,8192]{1,0:T(8,128)} %copy-done.6) | copy-start | bytes 3145732 | tf_op jit(solution)/shard_map/while
  730.2 34.0 %copy-start.21 = (f32[8192]{0:T(1024)S(1)}, f32[8192]{0:T(1024)}, u32[]{:S(2)}) copy-start(f32[8192]{0:T(1024)} %get-tuple-element.1232) | copy-start | bytes 98308 | tf_op jit(solution)/shard_map/while
  775.4 202.8 %copy-start.18 = (f32[64,32]{1,0:T(8,128)S(1)}, f32[64,32]{1,0:T(8,128)}, u32[]{:S(2)}) copy-start(f32[64,32]{1,0:T(8,128)} %copy-done.17) | copy-start | bytes 24580
  775.4 202.8 %copy-start.11 = (f32[64,8192]{1,0:T(8,128)S(1)}, f32[64,8192]{1,0:T(8,128)}, u32[]{:S(2)}) copy-start(f32[64,8192]{1,0:T(8,128)} %get-tuple-element.1276) | copy-start | bytes 6291460
  777.5 11.6 %collective-permute-start = (f32[16,8192]{1,0:T(8,128)}, f32[16,8192]{1,0:T(8,128)S(1)}, u32[]{:S(2)}, u32[]{:S(2)}) collective-permute-start(f32[16,8192]{1,0:T(8,128)} %multiply_add_fusion.5), channel_id=1, source_target_pairs={{0,2},{2,4},{4,6},{6,8},{8,10},{10,12},{12,14},{14,16},{16,18},{18... | collective-permute-start | bytes 1572872 | tf_op jit(solution)/shard_map/while/body/eval_jaxpr/ppermute | solution.py:18
  791.0 11.6 %collective-permute-start = (f32[16,8192]{1,0:T(8,128)}, f32[16,8192]{1,0:T(8,128)S(1)}, u32[]{:S(2)}, u32[]{:S(2)}) collective-permute-start(f32[16,8192]{1,0:T(8,128)} %multiply_add_fusion.5), channel_id=1, source_target_pairs={{0,2},{2,4},{4,6},{6,8},{8,10},{10,12},{12,14},{14,16},{16,18},{18... | collective-permute-start | bytes 1572872 | tf_op jit(solution)/shard_map/while/body/eval_jaxpr/ppermute | solution.py:18
  804.5 11.6 %collective-permute-start = (f32[16,8192]{1,0:T(8,128)}, f32[16,8192]{1,0:T(8,128)S(1)}, u32[]{:S(2)}, u32[]{:S(2)}) collective-permute-start(f32[16,8192]{1,0:T(8,128)} %multiply_add_fusion.5), channel_id=1, source_target_pairs={{0,2},{2,4},{4,6},{6,8},{8,10},{10,12},{12,14},{14,16},{16,18},{18... | collective-permute-start | bytes 1572872 | tf_op jit(solution)/shard_map/while/body/eval_jaxpr/ppermute | solution.py:18
  818.0 11.6 %collective-permute-start = (f32[16,8192]{1,0:T(8,128)}, f32[16,8192]{1,0:T(8,128)S(1)}, u32[]{:S(2)}, u32[]{:S(2)}) collective-permute-start(f32[16,8192]{1,0:T(8,128)} %multiply_add_fusion.5), channel_id=1, source_target_pairs={{0,2},{2,4},{4,6},{6,8},{8,10},{10,12},{12,14},{14,16},{16,18},{18... | collective-permute-start | bytes 1572872 | tf_op jit(solution)/shard_map/while/body/eval_jaxpr/ppermute | solution.py:18
  831.5 11.6 %collective-permute-start = (f32[16,8192]{1,0:T(8,128)}, f32[16,8192]{1,0:T(8,128)S(1)}, u32[]{:S(2)}, u32[]{:S(2)}) collective-permute-start(f32[16,8192]{1,0:T(8,128)} %multiply_add_fusion.5), channel_id=1, source_target_pairs={{0,2},{2,4},{4,6},{6,8},{8,10},{10,12},{12,14},{14,16},{16,18},{18... | collective-permute-start | bytes 1572872 | tf_op jit(solution)/shard_map/while/body/eval_jaxpr/ppermute | solution.py:18
  845.0 11.6 %collective-permute-start = (f32[16,8192]{1,0:T(8,128)}, f32[16,8192]{1,0:T(8,128)S(1)}, u32[]{:S(2)}, u32[]{:S(2)}) collective-permute-start(f32[16,8192]{1,0:T(8,128)} %multiply_add_fusion.5), channel_id=1, source_target_pairs={{0,2},{2,4},{4,6},{6,8},{8,10},{10,12},{12,14},{14,16},{16,18},{18... | collective-permute-start | bytes 1572872 | tf_op jit(solution)/shard_map/while/body/eval_jaxpr/ppermute | solution.py:18
  858.6 11.6 %collective-permute-start = (f32[16,8192]{1,0:T(8,128)}, f32[16,8192]{1,0:T(8,128)S(1)}, u32[]{:S(2)}, u32[]{:S(2)}) collective-permute-start(f32[16,8192]{1,0:T(8,128)} %multiply_add_fusion.5), channel_id=1, source_target_pairs={{0,2},{2,4},{4,6},{6,8},{8,10},{10,12},{12,14},{14,16},{16,18},{18... | collective-permute-start | bytes 1572872 | tf_op jit(solution)/shard_map/while/body/eval_jaxpr/ppermute | solution.py:18
  872.1 11.6 %collective-permute-start = (f32[16,8192]{1,0:T(8,128)}, f32[16,8192]{1,0:T(8,128)S(1)}, u32[]{:S(2)}, u32[]{:S(2)}) collective-permute-start(f32[16,8192]{1,0:T(8,128)} %multiply_add_fusion.5), channel_id=1, source_target_pairs={{0,2},{2,4},{4,6},{6,8},{8,10},{10,12},{12,14},{14,16},{16,18},{18... | collective-permute-start | bytes 1572872 | tf_op jit(solution)/shard_map/while/body/eval_jaxpr/ppermute | solution.py:18
  885.6 11.6 %collective-permute-start = (f32[16,8192]{1,0:T(8,128)}, f32[16,8192]{1,0:T(8,128)S(1)}, u32[]{:S(2)}, u32[]{:S(2)}) collective-permute-start(f32[16,8192]{1,0:T(8,128)} %multiply_add_fusion.5), channel_id=1, source_target_pairs={{0,2},{2,4},{4,6},{6,8},{8,10},{10,12},{12,14},{14,16},{16,18},{18... | collective-permute-start | bytes 1572872 | tf_op jit(solution)/shard_map/while/body/eval_jaxpr/ppermute | solution.py:18
  899.1 11.6 %collective-permute-start = (f32[16,8192]{1,0:T(8,128)}, f32[16,8192]{1,0:T(8,128)S(1)}, u32[]{:S(2)}, u32[]{:S(2)}) collective-permute-start(f32[16,8192]{1,0:T(8,128)} %multiply_add_fusion.5), channel_id=1, source_target_pairs={{0,2},{2,4},{4,6},{6,8},{8,10},{10,12},{12,14},{14,16},{16,18},{18... | collective-permute-start | bytes 1572872 | tf_op jit(solution)/shard_map/while/body/eval_jaxpr/ppermute | solution.py:18
  912.6 11.6 %collective-permute-start = (f32[16,8192]{1,0:T(8,128)}, f32[16,8192]{1,0:T(8,128)S(1)}, u32[]{:S(2)}, u32[]{:S(2)}) collective-permute-start(f32[16,8192]{1,0:T(8,128)} %multiply_add_fusion.5), channel_id=1, source_target_pairs={{0,2},{2,4},{4,6},{6,8},{8,10},{10,12},{12,14},{14,16},{16,18},{18... | collective-permute-start | bytes 1572872 | tf_op jit(solution)/shard_map/while/body/eval_jaxpr/ppermute | solution.py:18
  926.1 11.6 %collective-permute-start = (f32[16,8192]{1,0:T(8,128)}, f32[16,8192]{1,0:T(8,128)S(1)}, u32[]{:S(2)}, u32[]{:S(2)}) collective-permute-start(f32[16,8192]{1,0:T(8,128)} %multiply_add_fusion.5), channel_id=1, source_target_pairs={{0,2},{2,4},{4,6},{6,8},{8,10},{10,12},{12,14},{14,16},{16,18},{18... | collective-permute-start | bytes 1572872 | tf_op jit(solution)/shard_map/while/body/eval_jaxpr/ppermute | solution.py:18
  939.6 11.6 %collective-permute-start = (f32[16,8192]{1,0:T(8,128)}, f32[16,8192]{1,0:T(8,128)S(1)}, u32[]{:S(2)}, u32[]{:S(2)}) collective-permute-start(f32[16,8192]{1,0:T(8,128)} %multiply_add_fusion.5), channel_id=1, source_target_pairs={{0,2},{2,4},{4,6},{6,8},{8,10},{10,12},{12,14},{14,16},{16,18},{18... | collective-permute-start | bytes 1572872 | tf_op jit(solution)/shard_map/while/body/eval_jaxpr/ppermute | solution.py:18
  953.1 11.6 %collective-permute-start = (f32[16,8192]{1,0:T(8,128)}, f32[16,8192]{1,0:T(8,128)S(1)}, u32[]{:S(2)}, u32[]{:S(2)}) collective-permute-start(f32[16,8192]{1,0:T(8,128)} %multiply_add_fusion.5), channel_id=1, source_target_pairs={{0,2},{2,4},{4,6},{6,8},{8,10},{10,12},{12,14},{14,16},{16,18},{18... | collective-permute-start | bytes 1572872 | tf_op jit(solution)/shard_map/while/body/eval_jaxpr/ppermute | solution.py:18
  966.6 11.6 %collective-permute-start = (f32[16,8192]{1,0:T(8,128)}, f32[16,8192]{1,0:T(8,128)S(1)}, u32[]{:S(2)}, u32[]{:S(2)}) collective-permute-start(f32[16,8192]{1,0:T(8,128)} %multiply_add_fusion.5), channel_id=1, source_target_pairs={{0,2},{2,4},{4,6},{6,8},{8,10},{10,12},{12,14},{14,16},{16,18},{18... | collective-permute-start | bytes 1572872 | tf_op jit(solution)/shard_map/while/body/eval_jaxpr/ppermute | solution.py:18
  1002.1 13.0 %all-to-all-start.2 = ((bf16[2,32,8192]{2,1,0:T(8,128)(2,1)}), bf16[2,32,8192]{2,1,0:T(8,128)(2,1)S(1)}, u32[]{:S(2)}, u32[]{:S(2)}) async-start(bf16[2,32,8192]{2,1,0:T(8,128)(2,1)} %bitcast.19), calls=%async_computation.2 | async-start | bytes 2097152 | tf_op jit(solution)/shard_map/all_to_all | solution.py:195
  (38 other events, 281.4 us)
Sparse Core Ops, SparseCore 0:
  39.3 20.1 all-reduce.21
Sparse Core Ops, SparseCore 1:
  41.8 35.6 all-gather.2
  79.5 37.0 all-gather.4
where the time goes:
time: 1060 us; the launch traced here: 1040 us
  other arithmetic  447 us (42%)
  local copies, waits for them, and re-layouts  329 us (31%)
  waiting for transfers between devices  161 us (15%)
  starting transfers between devices  38.7 us (4%)
  blocking collectives  27.9 us (3%)
  between operations  16 us (2%)
  matrix products  14.5 us (1%)
    pad x32, local copies, waits for them, and re-layouts, local_one_block(): lax.associative_scan(scan_pair, (decays, pushes), axis=0)  286 us
    ppermute x16, waiting for transfers between devices, passed_along(): return lax.ppermute(array, axis, pairs)  150 us
    add x16, other arithmetic, scan_pair(): return (earlier[0] * later[0], later[0] * earlier[1] + later[1])  139 us
    add x16, other arithmetic, local_one_block(): lax.associative_scan(scan_pair, (decays, pushes), axis=0)  81.9 us
    reduce_sum x2, other arithmetic, local_one_block(): block_out = jnp.sum(output_mix[:, :, None] * states, axis=1)  60.4 us
    concatenate x16, other arithmetic, local_one_block(): lax.associative_scan(scan_pair, (decays, pushes), axis=0)  56 us
    ppermute x16, starting transfers between devices, passed_along(): return lax.ppermute(array, axis, pairs)  30.5 us
    add x15, other arithmetic, relay_step(): return passed_along(whole_decay * incoming + end_state, 'ctx', 1)  28.8 us
  transfers between devices with their start and end apart: 21, of which 18 were waited for; matrix products, arithmetic and copies ran while one was open for 73% of the time, Pallas kernels for 0%

commit v1 on v0

v1 whole, which is shorter than its diff:
```python
import functools
import math

import jax
import jax.numpy as jnp
from jax import lax
from jax.experimental import pallas as pl
from jax.experimental.pallas import tpu as pltpu
from jax.sharding import PartitionSpec as P

STATE = 16
CONV = 4
HEADS = 64
KV_HEADS = 8
HEAD_DIM = 128


def passed_along(array, axis, by):
    size = lax.axis_size(axis)
    pairs = [(i, i + by) for i in range(size) if 0 <= i + by < size]
    return lax.ppermute(array, axis, pairs)


LANES = 128
SUBS = 8
TILE = LANES * SUBS
LOG2E = math.log2(math.e)
MESH = pl.DeviceIdType.MESH


def to_rows(dst_ref, value):
    rows = value.shape[0]
    for sub in range(SUBS):
        dst_ref[pl.ds(sub, rows, stride=SUBS), :] = value[:, sub * LANES : (sub + 1) * LANES]


def spread_terms(terms_ref, spread_ref, count):
    rows = terms_ref.shape[0]
    for n in range(count):
        spread_ref[n * rows : (n + 1) * rows, :] = jnp.broadcast_to(
            terms_ref[:, n : n + 1], (rows, LANES)
        )


def row_of(spread_ref, index):
    return spread_ref[pl.ds(index, SUBS, stride=0), :]


def first_pass(low_ref, up_ref, bias_ref, act_ref, terms_ref, decay_ref,
               step_ref, end_ref, total_ref, spread, act_rows, rates):
    rows = act_ref.shape[0]

    @pl.when(pl.program_id(0) == 0)
    def _():
        spread_terms(terms_ref, spread, STATE)

    pre = jnp.dot(low_ref[...], up_ref[...], preferred_element_type=jnp.float32) + bias_ref[...]
    to_rows(step_ref.at[0], jax.nn.softplus(pre))
    to_rows(act_rows, act_ref[...].astype(jnp.float32))
    to_rows(rates, decay_ref[...] * (-LOG2E))
    rate = [rates[n * SUBS : (n + 1) * SUBS, :] for n in range(STATE)]

    def token(t, carry):
        states, total = carry
        at = pl.multiple_of(t * SUBS, SUBS)
        step = step_ref[0, pl.ds(at, SUBS), :]
        push = step * act_rows[pl.ds(at, SUBS), :]
        states = tuple(
            jnp.exp2(step * rate[n]) * states[n] + push * row_of(spread, n * rows + t)
            for n in range(STATE)
        )
        return states, total + step

    zero = jnp.zeros((SUBS, LANES), jnp.float32)
    states, total = lax.fori_loop(0, rows, token, ((zero,) * STATE, zero), unroll=4)
    for n in range(STATE):
        end_ref[0, n] = states[n]
    total_ref[0] = total


def second_pass(step_ref, act_ref, terms_ref, decay_ref, incoming_ref, gate_ref, skip_ref,
                out_ref, spread, act_rows, rates, outs):
    rows = act_ref.shape[0]

    @pl.when(pl.program_id(0) == 0)
    def _():
        spread_terms(terms_ref, spread, 2 * STATE)

    to_rows(act_rows, act_ref[...].astype(jnp.float32))
    to_rows(rates, decay_ref[...] * (-LOG2E))
    rate = [rates[n * SUBS : (n + 1) * SUBS, :] for n in range(STATE)]

    def token(t, states):
        at = pl.multiple_of(t * SUBS, SUBS)
        step = step_ref[0, pl.ds(at, SUBS), :]
        push = step * act_rows[pl.ds(at, SUBS), :]
        new, parts = [], []
        for n in range(STATE):
            state = jnp.exp2(step * rate[n]) * states[n] + push * row_of(spread, n * rows + t)
            new.append(state)
            term = state * row_of(spread, (STATE + n) * rows + t)
            if n < 2:
                parts.append(term)
            else:
                parts[n % 2] = parts[n % 2] + term
        outs[pl.ds(at, SUBS), :] = parts[0] + parts[1]
        return tuple(new)

    lax.fori_loop(0, rows, token, tuple(incoming_ref[0, n] for n in range(STATE)), unroll=4)
    for sub in range(SUBS):
        cols = slice(sub * LANES, (sub + 1) * LANES)
        mixed = outs[pl.ds(sub, rows, stride=SUBS), :]
        mixed = mixed + skip_ref[:, cols] * act_ref[:, cols].astype(jnp.float32)
        mixed = mixed.astype(jnp.bfloat16).astype(jnp.float32)
        out_ref[:, cols] = (mixed * jax.nn.silu(gate_ref[:, cols].astype(jnp.float32))).astype(
            jnp.bfloat16
        )


def exchange(n_ctx, rows_state, rows_total, send_ref, rate_ref, back_ref,
             got, reply, send_sem, got_sem, reply_sem, back_sem):
    me = lax.axis_index("ctx")
    barrier = pltpu.get_barrier_semaphore()
    for k in range(1, n_ctx):
        peer = lax.rem(me + k, n_ctx)
        pl.semaphore_signal(barrier, inc=1, device_id={"ctx": peer}, device_id_type=MESH)
    pl.semaphore_wait(barrier, n_ctx - 1)

    def there(k):
        peer = lax.rem(me + k, n_ctx)
        return pltpu.make_async_remote_copy(
            src_ref=send_ref.at[peer], dst_ref=got.at[me], send_sem=send_sem.at[k],
            recv_sem=got_sem.at[k], device_id={"ctx": peer}, device_id_type=MESH)

    def back(k):
        peer = lax.rem(me + k, n_ctx)
        return pltpu.make_async_remote_copy(
            src_ref=reply.at[peer], dst_ref=back_ref.at[me], send_sem=reply_sem.at[k],
            recv_sem=back_sem.at[k], device_id={"ctx": peer}, device_id_type=MESH)

    for k in range(1, n_ctx):
        there(k).start()
    got[me] = send_ref[me]
    for k in range(1, n_ctx):
        there(k).wait()

    state_shape = (rows_state, LANES)
    reps = rows_state // rows_total

    def combine(i, carry):
        sent = carry
        if reply.shape[1] > rows_state:
            spare = jnp.zeros((reply.shape[1] - rows_state, LANES), jnp.float32)
            sent = jnp.concatenate([carry, spare], axis=0)
        reply[i] = sent.astype(jnp.bfloat16)
        block = got[i].astype(jnp.float32)
        total = (block[rows_state : rows_state + rows_total]
                 + block[rows_state + rows_total : rows_state + 2 * rows_total])
        wide = jnp.concatenate([total] * reps, axis=0)
        return jnp.exp2(rate_ref[...] * wide) * carry + block[:rows_state]

    lax.fori_loop(0, n_ctx, combine, jnp.zeros(state_shape, jnp.float32))
    for k in range(1, n_ctx):
        back(k).start()
    back_ref[me] = reply[me]
    for k in range(1, n_ctx):
        back(k).wait()


def attend(queries, key_rows, value_rows):
    rows_here = queries.shape[0]
    groups_here = key_rows.shape[1] // HEAD_DIM
    group_size = HEADS // KV_HEADS
    scale_factor = 1.0 / math.sqrt(HEAD_DIM)
    query_heads = queries.reshape(rows_here, groups_here, group_size, HEAD_DIM)
    query_first = lax.axis_index("ctx") * rows_here
    query_pos = query_first + jnp.arange(rows_here, dtype=jnp.int32)
    initial = (
        jnp.full((groups_here, group_size, rows_here), -1e30, jnp.float32),
        jnp.zeros((groups_here, group_size, rows_here), jnp.float32),
        jnp.zeros((groups_here, group_size, rows_here, HEAD_DIM), jnp.float32),
    )
    key_piece = lax.all_gather(key_rows, "ctx", axis=0, tiled=True)
    value_piece = lax.all_gather(value_rows, "ctx", axis=0, tiled=True)
    piece_rows = key_piece.shape[0]
    block_len = math.gcd(piece_rows, 512)

    def fold_one_block(block_index, inner_state):
        block_first = block_index * block_len
        key_block = lax.dynamic_slice_in_dim(
            key_piece, block_index * block_len, block_len, 0
        ).reshape(block_len, groups_here, HEAD_DIM)
        value_block = lax.dynamic_slice_in_dim(
            value_piece, block_index * block_len, block_len, 0
        ).reshape(block_len, groups_here, HEAD_DIM)

        def visit(visit_state):
            running_max, running_total, running_sum = visit_state
            scores = (
                jnp.einsum(
                    "tkgd,skd->kgts", query_heads, key_block, preferred_element_type=jnp.float32
                )
                * scale_factor
            )
            visible = (block_first + jnp.arange(block_len, dtype=jnp.int32))[None, :] <= query_pos[
                :, None
            ]
            masked = jnp.where(visible, scores, -1e30)
            new_max = jnp.maximum(running_max, jnp.max(masked, axis=3))
            weights = jnp.where(visible, jnp.exp(masked - new_max[..., None]), 0.0)
            rescale = jnp.exp(running_max - new_max)
            new_total = running_total * rescale + jnp.sum(weights, axis=3)
            new_sum = running_sum * rescale[..., None] + jnp.einsum(
                "kgts,skd->kgtd",
                weights.astype(jnp.bfloat16),
                value_block,
                preferred_element_type=jnp.float32,
            )
            return (new_max, new_total, new_sum)

        return lax.cond(
            block_first > query_first + rows_here - 1, lambda skipped: skipped, visit, inner_state
        )

    final_max, final_total, final_sum = lax.fori_loop(
        0, piece_rows // block_len, fold_one_block, initial
    )
    mixed = final_sum / final_total[..., None]
    return (
        mixed.transpose(2, 0, 1, 3)
        .reshape(rows_here, groups_here * group_size * HEAD_DIM)
        .astype(jnp.bfloat16)
    )


def local(
    mamba_input, mamba_gate, conv_weight, conv_bias, step_down, state_proj, step_up, step_bias,
    decay_rate, skip_gain, queries, key_rows, value_rows,
):
    n_ctx, n_ch = lax.axis_size("ctx"), lax.axis_size("ch")
    inner_in = lax.all_to_all(mamba_input, "ch", split_axis=1, concat_axis=0, tiled=True)
    inner_gate = lax.all_to_all(mamba_gate, "ch", split_axis=1, concat_axis=0, tiled=True)
    rows, channels = inner_in.shape
    rim_rows = passed_along(inner_in[rows - (CONV - 1) :], "ctx", 1)
    padded = jnp.concatenate([rim_rows, inner_in], axis=0).astype(jnp.float32)
    conv_sum = conv_bias[None, :] + sum(
        conv_weight[tap][None, :] * padded[tap : tap + rows] for tap in range(CONV)
    )
    activation = jax.nn.silu(conv_sum).astype(jnp.bfloat16)
    low_part = jnp.dot(activation, step_down, preferred_element_type=jnp.float32)
    term_part = jnp.dot(activation, state_proj, preferred_element_type=jnp.float32)
    part = jnp.concatenate([low_part, term_part], axis=1)
    part_b = part.astype(jnp.bfloat16)
    summed = part
    for by in range(1, n_ch):
        pairs = [(i, (i + by) % n_ch) for i in range(n_ch)]
        summed = summed + lax.ppermute(part_b, "ch", pairs).astype(jnp.float32)
    rank = step_down.shape[1]
    step_low = summed[:, :rank].astype(jnp.bfloat16)
    state_terms = summed[:, rank:]

    tiles = channels // TILE
    f32, bf16 = jnp.float32, jnp.bfloat16
    whole = lambda shape: pl.BlockSpec(shape, lambda i: (0,) * len(shape))
    cols = lambda r: pl.BlockSpec((r, TILE), lambda i: (0, i))
    tile_rows = rows * SUBS
    params = pltpu.CompilerParams(vmem_limit_bytes=32 * 1024 * 1024)
    step_rows, end_state, totals = pl.pallas_call(
        first_pass,
        grid=(tiles,),
        in_specs=[whole((rows, rank)), cols(rank), cols(1), cols(rows), whole((rows, 2 * STATE)),
                  cols(STATE)],
        out_specs=[
            pl.BlockSpec((1, tile_rows, LANES), lambda i: (i, 0, 0)),
            pl.BlockSpec((1, STATE, SUBS, LANES), lambda i: (i, 0, 0, 0)),
            pl.BlockSpec((1, SUBS, LANES), lambda i: (i, 0, 0)),
        ],
        out_shape=[
            jax.ShapeDtypeStruct((tiles, tile_rows, LANES), f32),
            jax.ShapeDtypeStruct((tiles, STATE, SUBS, LANES), f32),
            jax.ShapeDtypeStruct((tiles, SUBS, LANES), f32),
        ],
        scratch_shapes=[
            pltpu.VMEM((STATE * rows, LANES), f32),
            pltpu.VMEM((tile_rows, LANES), f32),
            pltpu.VMEM((STATE * SUBS, LANES), f32),
        ],
        compiler_params=params,
        name="first_pass",
    )(step_low, step_up, step_bias[None], activation, state_terms, decay_rate)

    splits = max(1, n_ctx * LANES // channels)
    groups, held = n_ctx // splits, STATE // splits
    chunk = channels // groups
    subs = chunk // LANES
    per_tile = SUBS // subs
    rows_state = held * subs
    rows_back = -(-rows_state // 16) * 16
    rows_all = -(-(rows_state + 2 * subs) // 16) * 16
    ends = end_state.reshape(tiles, splits, held, per_tile, subs, LANES).transpose(0, 3, 1, 2, 4, 5)
    ends = ends.reshape(n_ctx, rows_state, LANES).astype(bf16)
    total = jnp.repeat(totals.reshape(groups, subs, LANES), splits, axis=0)
    total_hi = total.astype(bf16)
    total_lo = (total - total_hi.astype(f32)).astype(bf16)
    fill = jnp.zeros((n_ctx, rows_all - rows_state - 2 * subs, LANES), bf16)
    packed = jnp.concatenate([ends, total_hi, total_lo, fill], axis=1)
    me = lax.axis_index("ctx")
    my_rate = lax.dynamic_slice(
        decay_rate, (me % splits * held, me // splits * chunk), (held, chunk))
    my_rate = (my_rate * (-LOG2E)).reshape(rows_state, LANES)
    incoming = pl.pallas_call(
        functools.partial(exchange, n_ctx, rows_state, subs),
        in_specs=[pl.BlockSpec(memory_space=pltpu.VMEM)] * 2,
        out_specs=pl.BlockSpec(memory_space=pltpu.VMEM),
        out_shape=jax.ShapeDtypeStruct((n_ctx, rows_back, LANES), bf16),
        scratch_shapes=[
            pltpu.VMEM((n_ctx, rows_all, LANES), bf16),
            pltpu.VMEM((n_ctx, rows_back, LANES), bf16),
        ] + [pltpu.SemaphoreType.DMA((n_ctx,))] * 4,
        compiler_params=pltpu.CompilerParams(
            collective_id=0, has_side_effects=True, vmem_limit_bytes=32 * 1024 * 1024),
        name="exchange",
    )(packed, my_rate)
    incoming = incoming[:, :rows_state].reshape(tiles, per_tile, splits, held, subs, LANES)
    incoming = incoming.transpose(0, 2, 3, 1, 4, 5)
    incoming = incoming.reshape(tiles, STATE, SUBS, LANES).astype(f32)

    outgoing = pl.pallas_call(
        second_pass,
        grid=(tiles,),
        in_specs=[
            pl.BlockSpec((1, tile_rows, LANES), lambda i: (i, 0, 0)),
            cols(rows), whole((rows, 2 * STATE)), cols(STATE),
            pl.BlockSpec((1, STATE, SUBS, LANES), lambda i: (i, 0, 0, 0)),
            cols(rows), cols(1),
        ],
        out_specs=cols(rows),
        out_shape=jax.ShapeDtypeStruct((rows, channels), bf16),
        scratch_shapes=[
            pltpu.VMEM((2 * STATE * rows, LANES), f32),
            pltpu.VMEM((tile_rows, LANES), f32),
            pltpu.VMEM((STATE * SUBS, LANES), f32),
            pltpu.VMEM((tile_rows, LANES), f32),
        ],
        compiler_params=params,
        name="second_pass",
    )(step_rows, activation, state_terms, decay_rate, incoming, inner_gate, skip_gain[None])
    mamba_out = lax.all_to_all(outgoing, "ch", split_axis=0, concat_axis=1, tiled=True)
    attention_out = attend(queries, key_rows, value_rows)
    return (mamba_out, attention_out)


def solution(mesh):
    placed = (
        P(("ctx", "ch"), None),
        P(("ctx", "ch"), None),
        P(None, "ch"),
        P("ch"),
        P("ch", None),
        P("ch", None),
        P(None, "ch"),
        P("ch"),
        P(None, "ch"),
        P("ch"),
        P("ctx", "ch"),
        P("ctx", "ch"),
        P("ctx", "ch"),
    )
    return jax.shard_map(
        local,
        mesh=mesh,
        in_specs=placed,
        out_specs=(P(("ctx", "ch"), None), P("ctx", "ch")),
        check_vma=False,
    )
```

time: 1060 us -> 149 us (0.14); the launches traced: 1040 us -> 148 us
  other arithmetic: 447 us -> 6.95 us
  local copies, waits for them, and re-layouts: 329 us -> 20.5 us
  waiting for transfers between devices: 161 us -> 36.5 us
  Pallas kernels: 0 us -> 45.1 us
  blocking collectives: 27.9 us -> 0 us
  starting transfers between devices: 38.7 us -> 14.6 us
    pad x32 -> x0, local copies, waits for them, and re-layouts: 286 us -> none  [local_one_block(): lax.associative_scan(scan_pair, (decays, pushes), axis=0)]
    add x47 -> x1, other arithmetic: 250 us -> 0.02 us  [local(): summed = summed + lax.ppermute(part_b, 'ch', pairs).astype(jnp.float32)]
    ppermute x16 -> x1, waiting for transfers between devices: 150 us -> 5.95 us  [passed_along(): return lax.ppermute(array, axis, pairs)]
    reduce_sum x4 -> x0, other arithmetic: 73.3 us -> none  [the longest x2 60.4 us: local_one_block(): block_out = jnp.sum(output_mix[:, :, None] * states, axis=1)]
    concatenate x16 -> x1, other arithmetic: 56 us -> 0.14 us  [local(): packed = jnp.concatenate([ends, total_hi, total_lo, fill], axis=1)]
    pallas_call x0 -> x3, Pallas kernels: none -> 45.1 us  [the longest x1 21.9 us: local(): pl.pallas_call(functools.partial(exchange, n_ctx, rows_state, subs), in_s...]
    ppermute x16 -> x1, starting transfers between devices: 30.5 us -> 1.92 us  [passed_along(): return lax.ppermute(array, axis, pairs)]
    mul x4 -> x1, other arithmetic: 19.3 us -> 0.01 us  [local(): my_rate = (my_rate * -LOG2E).reshape(rows_state, LANES)]
  transfers between devices with their start and end apart: 21 -> 7, of which waited for: 18 -> 4; matrix products, arithmetic and copies ran while one was open for 73% -> 10% of each run, Pallas kernels for 0% -> 30%
where the time goes in v1:
time: 149 us; the launch traced here: 148 us
  Pallas kernels  45.1 us (30%)
  waiting for transfers between devices  36.5 us (24%)
  local copies, waits for them, and re-layouts  20.5 us (14%)
  starting transfers between devices  14.6 us (10%)
  between operations  14.4 us (10%)
  matrix products  10.2 us (7%)
  other arithmetic  6.95 us (5%)
    pallas_call x1, Pallas kernels, local(): pl.pallas_call(functools.partial(exchange, n_ctx, rows_state, subs), in_s...  21.9 us
    all_to_all x1, waiting for transfers between devices, local(): lax.all_to_all(outgoing, 'ch', split_axis=0, concat_axis=1, tiled=True)  14.2 us
    pallas_call x1, Pallas kernels, local(): pl.pallas_call(second_pass, grid=(tiles,), in_specs=[pl.BlockSpec((1, til...  12.1 us
    all_to_all x1, waiting for transfers between devices, local(): lax.all_to_all(mamba_input, 'ch', split_axis=1, concat_axis=0, tiled=True)  12 us
    unnamed x31, local copies, waits for them, and re-layouts  11.3 us
    pallas_call x1, Pallas kernels, local(): pl.pallas_call(first_pass, grid=(tiles,), in_specs=[whole((rows, rank)),...  11.1 us
    ppermute x1, waiting for transfers between devices, passed_along(): return lax.ppermute(array, axis, pairs)  5.95 us
    dot_general x1, matrix products, local(): jnp.dot(activation, step_down, preferred_element_type=jnp.float32)  5.02 us
  transfers between devices with their start and end apart: 7, of which 4 were waited for; matrix products, arithmetic and copies ran while one was open for 10% of the time, Pallas kernels for 30%

profile of v1, /device:TPU:16, one launch (start us, length us, event | category | flops | bytes accessed | tf_op | source)
XLA Modules:
  0.0 148.4 jit_solution(11864436516142308980)
XLA Ops:
  7.9 2.3 %copy.62 = bf16[4,2,8,8192]{3,2,0,1:T(8,128)(2,1)} copy(bf16[4,2,8,8192]{3,2,1,0:T(8,128)(2,1)} %bitcast.92) | data formatting | bytes 2097152 | tf_op jit(solution)/shard_map/all_to_all | solution.py:241
  10.2 3.6 %all-to-all-start = ((bf16[32,2,8192]{2,0,1:T(8,128)(2,1)}), bf16[32,2,8192]{2,0,1:T(8,128)(2,1)S(1)}, u32[]{:S(2)}, u32[]{:S(2)}) async-start(bf16[32,2,8192]{2,0,1:T(8,128)(2,1)} %bitcast.74), calls=%async_computation | async-start | bytes 2097152 | tf_op jit(solution)/shard_map/all_to_all | solution.py:241
  14.6 1.1 copy.61
  15.6 12.0 %all-to-all-done = bf16[32,2,8192]{2,0,1:T(8,128)(2,1)S(1)} async-done(((bf16[32,2,8192]{2,0,1:T(8,128)(2,1)}), bf16[32,2,8192]{2,0,1:T(8,128)(2,1)S(1)}, u32[]{:S(2)}, u32[]{:S(2)}) %all-to-all-start) | async-done | bytes 1048608 | tf_op jit(solution)/shard_map/all_to_all | solution.py:241
  27.6 3.6 %all-to-all-start.1 = ((bf16[32,2,8192]{2,0,1:T(8,128)(2,1)}), bf16[32,2,8192]{2,0,1:T(8,128)(2,1)S(1)}, u32[]{:S(2)}, u32[]{:S(2)}) async-start(bf16[32,2,8192]{2,0,1:T(8,128)(2,1)} %bitcast.87), calls=%async_computation.1 | async-start | bytes 2097152 | tf_op jit(solution)/shard_map/all_to_all | solution.py:242
  31.3 1.9 %collective-permute-start = (bf16[3,8192]{1,0:T(4,128)(2,1)S(1)}, bf16[3,8192]{1,0:T(4,128)(2,1)S(1)}, u32[]{:S(2)}, u32[]{:S(2)}) collective-permute-start(bf16[3,8192]{1,0:T(4,128)(2,1)S(1)} %slice.45), channel_id=1, source_target_pairs={{0,2},{2,4},{4,6},{6,8},{8,10},{10,12},{12,14},{14,16},{16,18},{18... | collective-permute-start | bytes 147464 | tf_op jit(solution)/shard_map/ppermute | solution.py:21
  33.3 5.9 %collective-permute-done = bf16[3,8192]{1,0:T(4,128)(2,1)S(1)} collective-permute-done((bf16[3,8192]{1,0:T(4,128)(2,1)S(1)}, bf16[3,8192]{1,0:T(4,128)(2,1)S(1)}, u32[]{:S(2)}, u32[]{:S(2)}) %collective-permute-start) | collective-permute-done | bytes 49184 | tf_op jit(solution)/shard_map/ppermute | solution.py:21
  39.6 1.3 multiply_convert_fusion.act_ref
  41.4 5.0 %fusion.21 = f32[64,512]{1,0:T(8,128)S(1)} fusion(bf16[64,8192]{1,0:T(8,128)(2,1)S(1)} %multiply_convert_fusion.act_ref, bf16[8192,512]{1,0:T(8,128)(2,1)} %param.21), kind=kOutput, calls=%fused_computation.42 | convolution fusion | flops 536870912 | bytes 9568256 | tf_op jit(solution)/shard_map/dot_general | solution.py:250
  47.0 1.6 %collective-permute-start.1 = (bf16[64,544]{1,0:T(8,128)(2,1)}, bf16[64,544]{1,0:T(8,128)(2,1)S(1)}, u32[]{:S(2)}, u32[]{:S(2)}) collective-permute-start(bf16[64,544]{1,0:T(8,128)(2,1)} %fusion.19), channel_id=1, source_target_pairs={{0,1},{1,0},{2,3},{3,2},{4,5},{5,4},{6,7},{7,6},{8,9},{9,8},{10,11... | collective-permute-start | bytes 208904 | tf_op jit(solution)/shard_map/ppermute | solution.py:257
  48.7 3.0 %collective-permute-done.1 = bf16[64,544]{1,0:T(8,128)(2,1)S(1)} collective-permute-done((bf16[64,544]{1,0:T(8,128)(2,1)}, bf16[64,544]{1,0:T(8,128)(2,1)S(1)}, u32[]{:S(2)}, u32[]{:S(2)}) %collective-permute-start.1) | collective-permute-done | bytes 69664 | tf_op jit(solution)/shard_map/ppermute | solution.py:257
  51.8 3.4 %copy-done.1 = bf16[512,8192]{1,0:T(8,128)(2,1)S(1)} copy-done((bf16[512,8192]{1,0:T(8,128)(2,1)S(1)}, bf16[512,8192]{1,0:T(8,128)(2,1)}, u32[]{:S(2)}) %copy-start.1) | copy-done | bytes 8388632
  55.1 11.1 %first_pass.1 = (f32[8,512,128]{2,1,0:T(8,128)S(1)}, f32[8,16,8,128]{3,2,1,0:T(8,128)S(1)}, f32[8,8,128]{2,1,0:T(8,128)S(1)}) custom-call(bf16[64,512]{1,0:T(8,128)(2,1)S(1)} %slice.79.low_ref, bf16[512,8192]{1,0:T(8,128)(2,1)S(1)} %copy-done.1, f32[1,8192]{1,0:T(1,128)S(1)} %bitcast.80, bf16[64,8192]{1,0:T(8,128)(2,1)S(1)} %multiply_convert_fusion.act_ref, ...), custom_call_target="tpu_custom_call" | custom-call | tf_op jit(solution)/shard_map/first_pass/pallas_call | solution.py:268
  66.6 21.9 %exchange.1 = bf16[16,64,128]{2,1,0:T(8,128)(2,1)S(1)} custom-call(bf16[16,80,128]{2,1,0:T(8,128)(2,1)S(1)} %maximum_maximum_fusion.send_ref, f32[64,128]{1,0:T(8,128)S(1)} %reshape.64.rate_ref), custom_call_target="tpu_custom_call" | custom-call | tf_op jit(solution)/shard_map/exchange/pallas_call | solution.py:311
  89.3 1.6 %copy-done.5 = f32[8,512,128]{2,1,0:T(8,128)S(1)} copy-done((f32[8,512,128]{2,1,0:T(8,128)S(1)}, f32[8,512,128]{2,1,0:T(8,128)}, u32[]{:S(2)}) %copy-start.5) | copy-done | bytes 2097176
  90.9 1.0 copy-done.6
  91.9 12.1 %second_pass.1 = bf16[64,8192]{1,0:T(8,128)(2,1)S(1)} custom-call(f32[8,512,128]{2,1,0:T(8,128)S(1)} %copy-done.5, bf16[64,8192]{1,0:T(8,128)(2,1)S(1)} %multiply_convert_fusion.act_ref, f32[64,32]{1,0:T(8,128)S(1)} %slice.51.terms_ref, f32[16,8192]{1,0:T(8,128)S(1)} %copy-done.3, f32[8,16,8,128]{3,2,1,0:T(8,128)S(1)} %bitcast.78, ...), custom_call_target="tpu_custom_call" | custom-call | tf_op jit(solution)/shard_map/second_pass/pallas_call | solution.py:328
  105.1 3.9 %all-to-all-start.2 = ((bf16[2,32,8192]{2,1,0:T(8,128)(2,1)}), bf16[2,32,8192]{2,1,0:T(8,128)(2,1)S(1)}, u32[]{:S(2)}, u32[]{:S(2)}) async-start(bf16[2,32,8192]{2,1,0:T(8,128)(2,1)} %bitcast.77), calls=%async_computation.2 | async-start | bytes 2097152 | tf_op jit(solution)/shard_map/all_to_all | solution.py:348
  109.3 14.2 %all-to-all-done.2 = bf16[2,32,8192]{2,1,0:T(8,128)(2,1)S(1)} async-done(((bf16[2,32,8192]{2,1,0:T(8,128)(2,1)}), bf16[2,32,8192]{2,1,0:T(8,128)(2,1)S(1)}, u32[]{:S(2)}, u32[]{:S(2)}) %all-to-all-start.2) | async-done | bytes 1048608 | tf_op jit(solution)/shard_map/all_to_all | solution.py:348
  123.5 1.0 copy.55
  124.5 1.5 copy.42
  126.0 1.5 %copy.44 = bf16[1024,512]{0,1:T(8,128)(2,1)S(1)} copy(bf16[1024,512]{1,0:T(8,128)(2,1)} %all-gather.5.cloned.1.call-done) | data formatting | bytes 2097152
  127.6 1.1 broadcast_in_dim.50
  128.7 10.0 %while.20 = (s32[]{:T(128)}, f32[4,8,64]{2,1,0:T(8,128)S(1)}, f32[4,8,64]{2,1,0:T(8,128)S(1)}, f32[4,8,64,128]{3,2,1,0:T(8,128)}, s32[]{:T(128)}, /*index=5*/bf1...) while((s32[]{:T(128)}, f32[4,8,64]{2,1,0:T(8,128)S(1)}, ...), condition=%wide.region_5.6_spmd.clone, body=%wide.region_0.5_spmd.clone.sunk | while | flops 551064128 | bytes 27006316 | solution.py:225
  128.7 5.0 %conditional.3 = (f32[4,8,64]{2,1,0:T(8,128)S(1)}, f32[4,8,64]{2,1,0:T(8,128)S(1)}, f32[4,8,64,128]{3,2,1,0:T(8,128)}) conditional(s32[]{:T(128)} %convert_element_type.104, (s32[]{:T(128)}, s32[]{:T(128)}, bf16[1024,512]{0,1:T(8,128)(2,1)S(1)}, bf16[64,4,8,128]{3,0,2,1:T(8,128)(2,1)S(1)}, f32[4,8,64]{2,1,0:T(8,128)S(1)}, ...), branch_computations={%region_1.3_spmd, %region_4.4_spmd} | conditional | flops 551064128 | bytes 26989438 | solution.py:221
  129.7 1.3 fusion.4
  131.1 1.6 %fusion.8 = f32[4,8,64,128]{3,2,1,0:T(8,128)S(1)} fusion(bf16[512,4,128,1]{0,2,3,1:T(8,128)(2,1)S(1)} %bitcast.84, f32[4,512,64,8]{1,2,3,0:T(8,128)S(1)} %get-tuple-element.414, f32[4,8,64]{2,1,0:T(8,128)S(1)} %max.5, pred[64,512]{1,0:T(8,128)(4,1)S(1)} %broadcast_compare_fusion, f32[4,8,64,128]{3,2,1,0:T(8,128)S(1)} %copy-done.9, ...), kind=kOutput, calls=%fused_computation.8 | convolution fusion | flops 274202624 | bytes 6864896 | tf_op jit(solution)/shard_map/while/body/eval_jaxpr/cond/branch_0_fun/kgts,skd->kgtd/dot_general | solution.py:213
  133.6 5.0 %conditional.3 = (f32[4,8,64]{2,1,0:T(8,128)S(1)}, f32[4,8,64]{2,1,0:T(8,128)S(1)}, f32[4,8,64,128]{3,2,1,0:T(8,128)}) conditional(s32[]{:T(128)} %convert_element_type.104, (s32[]{:T(128)}, s32[]{:T(128)}, bf16[1024,512]{0,1:T(8,128)(2,1)S(1)}, bf16[64,4,8,128]{3,0,2,1:T(8,128)(2,1)S(1)}, f32[4,8,64]{2,1,0:T(8,128)S(1)}, ...), branch_computations={%region_1.3_spmd, %region_4.4_spmd} | conditional | flops 551064128 | bytes 26989438 | solution.py:221
  134.7 1.3 fusion.4
  136.1 1.6 %fusion.8 = f32[4,8,64,128]{3,2,1,0:T(8,128)S(1)} fusion(bf16[512,4,128,1]{0,2,3,1:T(8,128)(2,1)S(1)} %bitcast.84, f32[4,512,64,8]{1,2,3,0:T(8,128)S(1)} %get-tuple-element.414, f32[4,8,64]{2,1,0:T(8,128)S(1)} %max.5, pred[64,512]{1,0:T(8,128)(4,1)S(1)} %broadcast_compare_fusion, f32[4,8,64,128]{3,2,1,0:T(8,128)S(1)} %copy-done.9, ...), kind=kOutput, calls=%fused_computation.8 | convolution fusion | flops 274202624 | bytes 6864896 | tf_op jit(solution)/shard_map/while/body/eval_jaxpr/cond/branch_0_fun/kgts,skd->kgtd/dot_general | solution.py:213
  138.6 1.6 %fusion.18 = bf16[64,4,8,128]{3,0,2,1:T(8,128)(2,1)S(1)} fusion(f32[4,8,64,128]{3,2,1,0:T(8,128)} %get-tuple-element.344, f32[4,8,64]{2,1,0:T(8,128)S(1)} %get-tuple-element.345), kind=kLoop, calls=%fused_computation.33 | loop fusion | flops 524288 | bytes 1581056 | tf_op jit(solution)/shard_map/convert_element_type | solution.py:232
  140.6 1.0 copy.63
  (78 shorter events, 9.9 us)
Async XLA Ops:
  7.2 33.7 %copy-start = (bf16[8192,32]{0,1:T(8,128)(2,1)S(1)}, bf16[8192,32]{0,1:T(8,128)(2,1)}, u32[]{:S(2)}) copy-start(bf16[8192,32]{0,1:T(8,128)(2,1)} %param.22) | copy-start | bytes 1572868
  7.2 7.4 %copy-start.11 = (bf16[32,16384]{1,0:T(8,128)(2,1)S(1)}, bf16[32,16384]{1,0:T(8,128)(2,1)}, u32[]{:S(2)}) copy-start(bf16[32,16384]{1,0:T(8,128)(2,1)} %param.18) | copy-start | bytes 3145732
  7.2 117.3 %all-gather.3.cloned.1.call-start = ((), (), s32[]{:S(2)}) async-start(), calls=%async_computation.3 | async-start | bytes 1114112 | tf_op jit(solution)/shard_map/all_gather | solution.py:183
  10.2 17.4 %all-to-all-start = ((bf16[32,2,8192]{2,0,1:T(8,128)(2,1)}), bf16[32,2,8192]{2,0,1:T(8,128)(2,1)S(1)}, u32[]{:S(2)}, u32[]{:S(2)}) async-start(bf16[32,2,8192]{2,0,1:T(8,128)(2,1)} %bitcast.74), calls=%async_computation | async-start | bytes 2097152 | tf_op jit(solution)/shard_map/all_to_all | solution.py:241
  13.8 19.4 %copy-start.13 = (f32[4,8192]{1,0:T(4,128)S(1)}, f32[4,8192]{1,0:T(4,128)}, u32[]{:S(2)}) copy-start(f32[4,8192]{1,0:T(4,128)} %param.19) | copy-start | bytes 393220
  13.8 112.2 %all-gather.5.cloned.1.call-start = ((), (), s32[]{:S(2)}) async-start(), calls=%async_computation.4 | async-start | bytes 1114112 | tf_op jit(solution)/shard_map/all_gather | solution.py:184
  27.6 61.7 %all-to-all-start.1 = ((bf16[32,2,8192]{2,0,1:T(8,128)(2,1)}), bf16[32,2,8192]{2,0,1:T(8,128)(2,1)S(1)}, u32[]{:S(2)}, u32[]{:S(2)}) async-start(bf16[32,2,8192]{2,0,1:T(8,128)(2,1)} %bitcast.87), calls=%async_computation.1 | async-start | bytes 2097152 | tf_op jit(solution)/shard_map/all_to_all | solution.py:242
  31.2 8.3 %copy-start.14 = (f32[8192]{0:T(1024)S(1)}, f32[8192]{0:T(1024)}, u32[]{:S(2)}) copy-start(f32[8192]{0:T(1024)} %param.20) | copy-start | bytes 98308
  31.3 8.0 %collective-permute-start = (bf16[3,8192]{1,0:T(4,128)(2,1)S(1)}, bf16[3,8192]{1,0:T(4,128)(2,1)S(1)}, u32[]{:S(2)}, u32[]{:S(2)}) collective-permute-start(bf16[3,8192]{1,0:T(4,128)(2,1)S(1)} %slice.45), channel_id=1, source_target_pairs={{0,2},{2,4},{4,6},{6,8},{8,10},{10,12},{12,14},{14,16},{16,18},{18... | collective-permute-start | bytes 147464 | tf_op jit(solution)/shard_map/ppermute | solution.py:21
  41.3 7.3 %copy-start.3 = (f32[16,8192]{1,0:T(8,128)S(1)}, f32[16,8192]{1,0:T(8,128)}, u32[]{:S(2)}) copy-start(f32[16,8192]{1,0:T(8,128)} %decay_ref.3) | copy-start | bytes 1572868
  41.4 10.4 %copy-start.7 = (f32[8192]{0:T(1024)S(1)}, f32[8192]{0:T(1024)}, u32[]{:S(2)}) copy-start(f32[8192]{0:T(1024)} %param.24) | copy-start | bytes 98308
  47.0 4.7 %collective-permute-start.1 = (bf16[64,544]{1,0:T(8,128)(2,1)}, bf16[64,544]{1,0:T(8,128)(2,1)S(1)}, u32[]{:S(2)}, u32[]{:S(2)}) collective-permute-start(bf16[64,544]{1,0:T(8,128)(2,1)} %fusion.19), channel_id=1, source_target_pairs={{0,1},{1,0},{2,3},{3,2},{4,5},{5,4},{6,7},{7,6},{8,9},{9,8},{10,11... | collective-permute-start | bytes 208904 | tf_op jit(solution)/shard_map/ppermute | solution.py:257
  51.8 3.4 %copy-start.1 = (bf16[512,8192]{1,0:T(8,128)(2,1)S(1)}, bf16[512,8192]{1,0:T(8,128)(2,1)}, u32[]{:S(2)}) copy-start(bf16[512,8192]{1,0:T(8,128)(2,1)} %up_ref.1) | copy-start | bytes 25165828
  66.2 22.2 %copy-start.4 = (f32[8,512,128]{2,1,0:T(8,128)}, f32[8,512,128]{2,1,0:T(8,128)S(1)}, u32[]{:S(2)}) copy-start(f32[8,512,128]{2,1,0:T(8,128)S(1)} %get-tuple-element.341.step_ref) | copy-start | bytes 6291460
  66.2 23.1 %copy-start.8 = (f32[8192]{0:T(1024)S(1)}, f32[8192]{0:T(1024)}, u32[]{:S(2)}) copy-start(f32[8192]{0:T(1024)} %param.26) | copy-start | bytes 98308
  89.3 1.6 %copy-start.5 = (f32[8,512,128]{2,1,0:T(8,128)S(1)}, f32[8,512,128]{2,1,0:T(8,128)}, u32[]{:S(2)}) copy-start(f32[8,512,128]{2,1,0:T(8,128)} %copy-done.4) | copy-start | bytes 6291460
  90.9 1.0 copy-start.6
  104.1 1.0 copy-start.2
  105.1 3.9 %copy-start.12 = (bf16[64,4096]{1,0:T(8,128)(2,1)S(1)}, bf16[64,4096]{1,0:T(8,128)(2,1)}, u32[]{:S(2)}) copy-start(bf16[64,4096]{1,0:T(8,128)(2,1)} %param.27) | copy-start | bytes 1572868
  105.1 18.4 %all-to-all-start.2 = ((bf16[2,32,8192]{2,1,0:T(8,128)(2,1)}), bf16[2,32,8192]{2,1,0:T(8,128)(2,1)S(1)}, u32[]{:S(2)}, u32[]{:S(2)}) async-start(bf16[2,32,8192]{2,1,0:T(8,128)(2,1)} %bitcast.77), calls=%async_computation.2 | async-start | bytes 2097152 | tf_op jit(solution)/shard_map/all_to_all | solution.py:348
  129.7 1.4 copy-start.9
  132.7 1.0 copy-start.10
  134.7 1.4 copy-start.9
  137.7 1.0 copy-start.10
Sparse Core Ops, SparseCore 0:
  10.2 37.8 all-gather.2
  50.2 39.6 all-gather.4

commit v2 on v1

v2 whole, which is shorter than its diff:
```python
import functools
import math

import jax
import jax.numpy as jnp
from jax import lax
from jax.experimental import pallas as pl
from jax.experimental.pallas import tpu as pltpu
from jax.sharding import PartitionSpec as P

STATE = 16
CONV = 4
HEADS = 64
KV_HEADS = 8
HEAD_DIM = 128


def halo(mamba_input, n_ctx, n_ch):
    width = mamba_input.shape[1] // n_ch
    tail = mamba_input[mamba_input.shape[0] - (CONV - 1) :]
    arrived = 0
    for j in range(n_ch):
        pairs = [(c * n_ch + n_ch - 1, (c + 1) * n_ch + j) for c in range(n_ctx - 1)]
        part = lax.ppermute(tail[:, j * width : (j + 1) * width], ("ctx", "ch"), pairs)
        arrived = arrived + part
    return arrived


LANES = 128
SUBS = 8
TILE = LANES * SUBS
LOG2E = math.log2(math.e)
MESH = pl.DeviceIdType.MESH


def to_rows(dst_ref, value):
    rows = value.shape[0]
    for sub in range(SUBS):
        dst_ref[pl.ds(sub, rows, stride=SUBS), :] = value[:, sub * LANES : (sub + 1) * LANES]


def spread_terms(terms_ref, spread_ref, count):
    rows = terms_ref.shape[0]
    for n in range(count):
        spread_ref[n * rows : (n + 1) * rows, :] = jnp.broadcast_to(
            terms_ref[:, n : n + 1], (rows, LANES)
        )


def row_of(spread_ref, index):
    return spread_ref[pl.ds(index, SUBS, stride=0), :]


def first_pass(packing, low_ref, up_ref, bias_ref, act_ref, terms_ref, decay_ref,
               step_ref, packed_ref, spread, act_rows, rates, pack):
    rows = act_ref.shape[0]

    @pl.when(pl.program_id(0) == 0)
    def _():
        spread_terms(terms_ref, spread, STATE)

    pre = jnp.dot(low_ref[...], up_ref[...], preferred_element_type=jnp.float32) + bias_ref[...]
    to_rows(step_ref.at[0], jax.nn.softplus(pre))
    to_rows(act_rows, act_ref[...].astype(jnp.float32))
    to_rows(rates, decay_ref[...] * (-LOG2E))
    rate = [rates[n * SUBS : (n + 1) * SUBS, :] for n in range(STATE)]

    def token(t, carry):
        states, total = carry
        at = pl.multiple_of(t * SUBS, SUBS)
        step = step_ref[0, pl.ds(at, SUBS), :]
        push = step * act_rows[pl.ds(at, SUBS), :]
        states = tuple(
            jnp.exp2(step * rate[n]) * states[n] + push * row_of(spread, n * rows + t)
            for n in range(STATE)
        )
        return states, total + step

    zero = jnp.zeros((SUBS, LANES), jnp.float32)
    states, total = lax.fori_loop(0, rows, token, ((zero,) * STATE, zero), unroll=4)
    splits, subs, held, rows_state = packing
    total_hi = total.astype(jnp.bfloat16).astype(jnp.float32)
    pack[...] = jnp.zeros_like(pack)
    for part in range(pack.shape[0]):
        cut = slice(part // splits * subs, (part // splits + 1) * subs)
        for n in range(held):
            pack[part, n * subs : (n + 1) * subs] = states[part % splits * held + n][cut]
        pack[part, rows_state : rows_state + subs] = total_hi[cut]
        pack[part, rows_state + subs : rows_state + 2 * subs] = (total - total_hi)[cut]
    packed_ref[...] = pack[...].astype(jnp.bfloat16)


def second_pass(packing, n_ch, step_ref, act_ref, terms_ref, decay_ref, incoming_ref, gate_ref, skip_ref,
                out_ref, spread, act_rows, rates, outs, entering, wide, outbox,
                keep_sem, send_sem, recv_sem):
    rows = act_ref.shape[0]
    splits, subs, held, rows_state = packing
    tile, tiles = pl.program_id(0), pl.num_programs(0)
    me = lax.axis_index("ch")
    here = outbox.shape[1]
    channels = outbox.shape[2]

    @pl.when(tile == 0)
    def _():
        barrier = pltpu.get_barrier_semaphore()
        for k in range(1, n_ch):
            peer = lax.rem(me + k, n_ch)
            pl.semaphore_signal(barrier, inc=1, device_id={"ch": peer}, device_id_type=MESH)
        pl.semaphore_wait(barrier, n_ch - 1)
        spread_terms(terms_ref, spread, 2 * STATE)

    to_rows(act_rows, act_ref[...].astype(jnp.float32))
    to_rows(rates, decay_ref[...] * (-LOG2E))
    rate = [rates[n * SUBS : (n + 1) * SUBS, :] for n in range(STATE)]

    def token(t, states):
        at = pl.multiple_of(t * SUBS, SUBS)
        step = step_ref[0, pl.ds(at, SUBS), :]
        push = step * act_rows[pl.ds(at, SUBS), :]
        new, parts = [], []
        for n in range(STATE):
            state = jnp.exp2(step * rate[n]) * states[n] + push * row_of(spread, n * rows + t)
            new.append(state)
            term = state * row_of(spread, (STATE + n) * rows + t)
            if n < 2:
                parts.append(term)
            else:
                parts[n % 2] = parts[n % 2] + term
        outs[pl.ds(at, SUBS), :] = parts[0] + parts[1]
        return tuple(new)

    wide[...] = incoming_ref[...].astype(jnp.float32)
    for part in range(wide.shape[0]):
        for n in range(held):
            row = (part % splits * held + n) * SUBS + part // splits * subs
            entering[row : row + subs, :] = wide[part, n * subs : (n + 1) * subs]
    start = tuple(entering[n * SUBS : (n + 1) * SUBS, :] for n in range(STATE))
    lax.fori_loop(0, rows, token, start, unroll=4)
    first = pl.multiple_of(tile * TILE, TILE)
    for sub in range(SUBS):
        cols = slice(sub * LANES, (sub + 1) * LANES)
        mixed = outs[pl.ds(sub, rows, stride=SUBS), :]
        mixed = mixed + skip_ref[:, cols] * act_ref[:, cols].astype(jnp.float32)
        mixed = mixed.astype(jnp.bfloat16).astype(jnp.float32)
        mixed = mixed * jax.nn.silu(gate_ref[:, cols].astype(jnp.float32))
        mixed = mixed.astype(jnp.bfloat16)
        at = pl.multiple_of(first + sub * LANES, LANES)
        for j in range(n_ch):
            outbox[j, :, pl.ds(at, LANES)] = mixed[j * here : (j + 1) * here]

    def keep(i):
        source = pl.multiple_of(i * TILE, TILE)
        target = pl.multiple_of(me * channels + i * TILE, TILE)
        return pltpu.make_async_copy(
            outbox.at[me, :, pl.ds(source, TILE)], out_ref.at[:, pl.ds(target, TILE)],
            keep_sem.at[i])

    def send(i, k):
        peer = lax.rem(me + k, n_ch)
        source = pl.multiple_of(i * TILE, TILE)
        target = pl.multiple_of(me * channels + i * TILE, TILE)
        return pltpu.make_async_remote_copy(
            src_ref=outbox.at[peer, :, pl.ds(source, TILE)],
            dst_ref=out_ref.at[:, pl.ds(target, TILE)],
            send_sem=send_sem.at[i, k], recv_sem=recv_sem.at[i, k],
            device_id={"ch": peer}, device_id_type=MESH)

    for k in range(1, n_ch):
        send(tile, k).start()
    keep(tile).start()

    @pl.when(tile == tiles - 1)
    def _():
        @pl.loop(0, tiles)
        def _(i):
            for k in range(1, n_ch):
                send(i, k).wait()
            keep(i).wait()


def exchange(n_ctx, rows_state, rows_total, send_ref, rate_ref, q_ref, k_ref, v_ref,
             back_ref, mixed_ref, got, reply, send_sem, got_sem, reply_sem, back_sem):
    me = lax.axis_index("ctx")
    rows = q_ref.shape[0]
    groups = k_ref.shape[1] // HEAD_DIM
    block = q_ref.shape[1] // groups

    def attend(g, carry):
        at = pl.ds(pl.multiple_of(g * HEAD_DIM, HEAD_DIM), HEAD_DIM)
        first = pl.multiple_of(g * block, HEAD_DIM)
        parts = attend_group(
            me * rows, rows, q_ref[:, pl.ds(first, block)], k_ref[:, at], v_ref[:, at])
        for h, part in enumerate(parts):
            mixed_ref[:, pl.ds(pl.multiple_of(first + h * HEAD_DIM, HEAD_DIM), HEAD_DIM)] = part
        return carry

    barrier = pltpu.get_barrier_semaphore()
    for k in range(1, n_ctx):
        peer = lax.rem(me + k, n_ctx)
        pl.semaphore_signal(barrier, inc=1, device_id={"ctx": peer}, device_id_type=MESH)
    pl.semaphore_wait(barrier, n_ctx - 1)

    def there(k):
        peer = lax.rem(me + k, n_ctx)
        return pltpu.make_async_remote_copy(
            src_ref=send_ref.at[peer], dst_ref=got.at[me], send_sem=send_sem.at[k],
            recv_sem=got_sem.at[k], device_id={"ctx": peer}, device_id_type=MESH)

    def back(k):
        peer = lax.rem(me + k, n_ctx)
        return pltpu.make_async_remote_copy(
            src_ref=reply.at[peer], dst_ref=back_ref.at[me], send_sem=reply_sem.at[k],
            recv_sem=back_sem.at[k], device_id={"ctx": peer}, device_id_type=MESH)

    for k in range(1, n_ctx):
        there(k).start()
    got[me] = send_ref[me]
    half = (groups + 1) // 2
    lax.fori_loop(0, half, attend, 0)
    for k in range(1, n_ctx):
        there(k).wait()

    state_shape = (rows_state, LANES)
    reps = rows_state // rows_total

    def combine(i, carry):
        sent = carry
        if reply.shape[1] > rows_state:
            spare = jnp.zeros((reply.shape[1] - rows_state, LANES), jnp.float32)
            sent = jnp.concatenate([carry, spare], axis=0)
        reply[i] = sent.astype(jnp.bfloat16)
        block = got[i].astype(jnp.float32)
        total = (block[rows_state : rows_state + rows_total]
                 + block[rows_state + rows_total : rows_state + 2 * rows_total])
        wide = jnp.concatenate([total] * reps, axis=0)
        return jnp.exp2(rate_ref[...] * wide) * carry + block[:rows_state]

    lax.fori_loop(0, n_ctx, combine, jnp.zeros(state_shape, jnp.float32))
    for k in range(1, n_ctx):
        back(k).start()
    back_ref[me] = reply[me]
    lax.fori_loop(half, groups, attend, 0)
    for k in range(1, n_ctx):
        back(k).wait()


def attend_group(query_first, rows, q, k, v):
    heads = q.shape[1] // HEAD_DIM
    stacked = jnp.concatenate(
        [q[:, h * HEAD_DIM : (h + 1) * HEAD_DIM] for h in range(heads)], axis=0
    )
    scores = lax.dot_general(
        stacked, k, (((1,), (1,)), ((), ())), preferred_element_type=jnp.float32
    ) * (LOG2E / math.sqrt(HEAD_DIM))
    query_pos = query_first + lax.broadcasted_iota(jnp.int32, scores.shape, 0) % rows
    visible = lax.broadcasted_iota(jnp.int32, scores.shape, 1) <= query_pos
    masked = jnp.where(visible, scores, -1e30)
    weights = jnp.exp2(masked - jnp.max(masked, axis=1, keepdims=True))
    total = jnp.sum(weights, axis=1, keepdims=True)
    mixed = jnp.dot(weights.astype(jnp.bfloat16), v, preferred_element_type=jnp.float32) / total
    mixed = mixed.astype(jnp.bfloat16)
    return [mixed[h * rows : (h + 1) * rows] for h in range(heads)]


def local(
    mamba_input, mamba_gate, conv_weight, conv_bias, step_down, state_proj, step_up, step_bias,
    decay_rate, skip_gain, queries, key_rows, value_rows,
):
    n_ctx, n_ch = lax.axis_size("ctx"), lax.axis_size("ch")
    keys = lax.all_gather(key_rows, "ctx", axis=0, tiled=True)
    values = lax.all_gather(value_rows, "ctx", axis=0, tiled=True)
    inner_in = lax.all_to_all(mamba_input, "ch", split_axis=1, concat_axis=0, tiled=True)
    inner_gate = lax.all_to_all(mamba_gate, "ch", split_axis=1, concat_axis=0, tiled=True)
    rows, channels = inner_in.shape
    rim_rows = halo(mamba_input, n_ctx, n_ch)
    padded = jnp.concatenate([rim_rows, inner_in], axis=0).astype(jnp.float32)
    conv_sum = conv_bias[None, :] + sum(
        conv_weight[tap][None, :] * padded[tap : tap + rows] for tap in range(CONV)
    )
    activation = jax.nn.silu(conv_sum).astype(jnp.bfloat16)
    low_part = jnp.dot(activation, step_down, preferred_element_type=jnp.float32)
    term_part = jnp.dot(activation, state_proj, preferred_element_type=jnp.float32)
    part = jnp.concatenate([low_part, term_part], axis=1)
    part_b = part.astype(jnp.bfloat16)
    summed = part
    for by in range(1, n_ch):
        pairs = [(i, (i + by) % n_ch) for i in range(n_ch)]
        summed = summed + lax.ppermute(part_b, "ch", pairs).astype(jnp.float32)
    rank = step_down.shape[1]
    step_low = summed[:, :rank].astype(jnp.bfloat16)
    state_terms = summed[:, rank:]

    tiles = channels // TILE
    f32, bf16 = jnp.float32, jnp.bfloat16
    whole = lambda shape: pl.BlockSpec(shape, lambda i: (0,) * len(shape))
    cols = lambda r: pl.BlockSpec((r, TILE), lambda i: (0, i))
    step_spec = pl.BlockSpec((1, rows * SUBS, LANES), lambda i: (i, 0, 0))
    limit = 32 * 1024 * 1024
    tile_rows = rows * SUBS
    splits = max(1, n_ctx * LANES // channels)
    groups, held = n_ctx // splits, STATE // splits
    chunk = channels // groups
    subs = chunk // LANES
    parts = n_ctx // tiles
    rows_state = held * subs
    rows_back = -(-rows_state // 16) * 16
    rows_all = -(-(rows_state + 2 * subs) // 16) * 16
    packing = (splits, subs, held, rows_state)
    step_rows, packed = pl.pallas_call(
        functools.partial(first_pass, packing),
        grid=(tiles,),
        in_specs=[whole((rows, rank)), cols(rank), cols(1), cols(rows), whole((rows, 2 * STATE)),
                  cols(STATE)],
        out_specs=[step_spec, pl.BlockSpec((parts, rows_all, LANES), lambda i: (i, 0, 0))],
        out_shape=[
            jax.ShapeDtypeStruct((tiles, tile_rows, LANES), f32),
            jax.ShapeDtypeStruct((n_ctx, rows_all, LANES), bf16),
        ],
        scratch_shapes=[
            pltpu.VMEM((STATE * rows, LANES), f32),
            pltpu.VMEM((tile_rows, LANES), f32),
            pltpu.VMEM((STATE * SUBS, LANES), f32),
            pltpu.VMEM((parts, rows_all, LANES), f32),
        ],
        compiler_params=pltpu.CompilerParams(vmem_limit_bytes=limit),
        name="first_pass",
    )(step_low, step_up, step_bias[None], activation, state_terms, decay_rate)

    me = lax.axis_index("ctx")
    my_rate = lax.dynamic_slice(
        decay_rate, (me % splits * held, me // splits * chunk), (held, chunk))
    my_rate = (my_rate * (-LOG2E)).reshape(rows_state, LANES)
    vmem = pl.BlockSpec(memory_space=pltpu.VMEM)
    incoming, attention_out = pl.pallas_call(
        functools.partial(exchange, n_ctx, rows_state, subs),
        in_specs=[vmem] * 5,
        out_specs=[vmem] * 2,
        out_shape=[
            jax.ShapeDtypeStruct((n_ctx, rows_back, LANES), bf16),
            jax.ShapeDtypeStruct(queries.shape, bf16),
        ],
        scratch_shapes=[
            pltpu.VMEM((n_ctx, rows_all, LANES), bf16),
            pltpu.VMEM((n_ctx, rows_back, LANES), bf16),
        ] + [pltpu.SemaphoreType.DMA((n_ctx,))] * 4,
        compiler_params=pltpu.CompilerParams(
            collective_id=0, has_side_effects=True, vmem_limit_bytes=limit),
        name="exchange",
    )(packed, my_rate, queries, keys, values)

    mamba_out = pl.pallas_call(
        functools.partial(second_pass, packing, n_ch),
        grid=(tiles,),
        in_specs=[
            step_spec, cols(rows), whole((rows, 2 * STATE)), cols(STATE),
            pl.BlockSpec((parts, rows_back, LANES), lambda i: (i, 0, 0)),
            cols(rows), cols(1),
        ],
        out_specs=pl.BlockSpec(memory_space=pl.ANY),
        out_shape=jax.ShapeDtypeStruct(mamba_input.shape, bf16),
        scratch_shapes=[
            pltpu.VMEM((2 * STATE * rows, LANES), f32),
            pltpu.VMEM((tile_rows, LANES), f32),
            pltpu.VMEM((STATE * SUBS, LANES), f32),
            pltpu.VMEM((tile_rows, LANES), f32),
            pltpu.VMEM((STATE * SUBS, LANES), f32),
            pltpu.VMEM((parts, rows_back, LANES), f32),
            pltpu.VMEM((n_ch, rows // n_ch, channels), bf16),
            pltpu.SemaphoreType.DMA((tiles,)),
            pltpu.SemaphoreType.DMA((tiles, n_ch)),
            pltpu.SemaphoreType.DMA((tiles, n_ch)),
        ],
        compiler_params=pltpu.CompilerParams(
            collective_id=1, has_side_effects=True, vmem_limit_bytes=limit),
        name="second_pass",
    )(step_rows, activation, state_terms, decay_rate, incoming, inner_gate, skip_gain[None])
    return (mamba_out, attention_out)


def solution(mesh):
    placed = (
        P(("ctx", "ch"), None),
        P(("ctx", "ch"), None),
        P(None, "ch"),
        P("ch"),
        P("ch", None),
        P("ch", None),
        P(None, "ch"),
        P("ch"),
        P(None, "ch"),
        P("ch"),
        P("ctx", "ch"),
        P("ctx", "ch"),
        P("ctx", "ch"),
    )
    return jax.shard_map(
        local,
        mesh=mesh,
        in_specs=placed,
        out_specs=(P(("ctx", "ch"), None), P("ctx", "ch")),
        check_vma=False,
    )
```

time: 149 us -> 142 us (0.953)
  other arithmetic: 6.95 us -> 1.69 us
  matrix products: 10.2 us -> 5.54 us
  starting transfers between devices: 14.6 us -> 11.3 us
  Pallas kernels: 45.1 us -> 47.8 us
  waiting for transfers between devices: 36.5 us -> 38.9 us
    all_gather x2, waiting for transfers between devices: 0.02 us -> 21 us  [the longest x1 21 us: local(): values = lax.all_gather(value_rows, 'ctx', axis=0, tiled=True)]
    all_to_all x1 -> x0, waiting for transfers between devices: 14.2 us -> none  [local(): lax.all_to_all(outgoing, 'ch', split_axis=0, concat_axis=1, tiled=True)]
    all_to_all x1, waiting for transfers between devices: 12 us -> 5.86 us  [local(): lax.all_to_all(mamba_input, 'ch', split_axis=1, concat_axis=0, tiled=True)]
    pallas_call x2, Pallas kernels: 23.2 us -> 28.5 us  [the longest x1 17.2 us: local(): pl.pallas_call(functools.partial(second_pass, packing, n_ch), grid=(tiles...]
    unnamed x31 -> x36, local copies, waits for them, and re-layouts: 11.3 us -> 16.4 us
    dot_general x4 -> x0, matrix products: 4.73 us -> none  [the longest x2 3.12 us: visit(): jnp.einsum('kgts,skd->kgtd', weights.astype(jnp.bfloat16), value_block, p...]
    ppermute x1, waiting for transfers between devices: 2.98 us -> 6.93 us  [local(): summed = summed + lax.ppermute(part_b, 'ch', pairs).astype(jnp.float32)]
    all_to_all x1 -> x0, starting transfers between devices: 3.89 us -> none  [local(): lax.all_to_all(outgoing, 'ch', split_axis=0, concat_axis=1, tiled=True)]
  transfers between devices with their start and end apart: 7 -> 7, of which waited for: 4 -> 4; matrix products, arithmetic and copies ran while one was open for 10% -> 8% of each run, Pallas kernels for 30% -> 22%
where the time goes in v2:
time: 142 us; the launch traced here: 140 us
  Pallas kernels  47.8 us (34%)
  waiting for transfers between devices  38.9 us (27%)
  local copies, waits for them, and re-layouts  21 us (15%)
  between operations  14.3 us (10%)
  starting transfers between devices  11.3 us (8%)
  matrix products  5.54 us (4%)
  other arithmetic  1.69 us (1%)
    all_gather x1, waiting for transfers between devices, local(): values = lax.all_gather(value_rows, 'ctx', axis=0, tiled=True)  21 us
    pallas_call x1, Pallas kernels, local(): pl.pallas_call(functools.partial(exchange, n_ctx, rows_state, subs), in_s...  19.3 us
    pallas_call x1, Pallas kernels, local(): pl.pallas_call(functools.partial(second_pass, packing, n_ch), grid=(tiles...  17.2 us
    unnamed x36, local copies, waits for them, and re-layouts  16.4 us
    pallas_call x1, Pallas kernels, local(): pl.pallas_call(functools.partial(first_pass, packing), grid=(tiles,), in_...  11.3 us
    ppermute x1, waiting for transfers between devices, local(): summed = summed + lax.ppermute(part_b, 'ch', pairs).astype(jnp.float32)  6.93 us
    all_to_all x1, waiting for transfers between devices, local(): lax.all_to_all(mamba_input, 'ch', split_axis=1, concat_axis=0, tiled=True)  5.86 us
    dot_general x1, matrix products, local(): jnp.dot(activation, step_down, preferred_element_type=jnp.float32)  5.12 us
  transfers between devices with their start and end apart: 7, of which 4 were waited for; matrix products, arithmetic and copies ran while one was open for 8% of the time, Pallas kernels for 22%

profile of v2, /device:TPU:16, one launch (start us, length us, event | category | flops | bytes accessed | tf_op | source)
XLA Modules:
  0.0 140.5 jit_solution(9479365594048727589)
XLA Ops:
  7.2 0.7 all-gather.3.cloned.1.call-update
  7.9 2.4 %copy.24 = bf16[4,2,8,8192]{3,2,0,1:T(8,128)(2,1)} copy(bf16[4,2,8,8192]{3,2,1,0:T(8,128)(2,1)} %bitcast.28) | data formatting | bytes 2097152 | tf_op jit(solution)/shard_map/all_to_all | solution.py:272
  10.3 3.6 %all-to-all-start = ((bf16[32,2,8192]{2,0,1:T(8,128)(2,1)}), bf16[32,2,8192]{2,0,1:T(8,128)(2,1)S(1)}, u32[]{:S(2)}, u32[]{:S(2)}) async-start(bf16[32,2,8192]{2,0,1:T(8,128)(2,1)} %bitcast.23), calls=%async_computation | async-start | bytes 2097152 | tf_op jit(solution)/shard_map/all_to_all | solution.py:272
  13.9 1.0 fusion.5
  15.0 1.3 collective-permute-start
  16.3 0.7 collective-permute-start.1
  17.1 1.1 copy.23
  18.2 4.3 %collective-permute-done = bf16[3,8192]{1,0:T(4,128)(2,1)S(1)} collective-permute-done((bf16[3,8192]{1,0:T(4,128)(2,1)S(1)}, bf16[3,8192]{1,0:T(4,128)(2,1)S(1)}, u32[]{:S(2)}, u32[]{:S(2)}) %collective-permute-start) | collective-permute-done | bytes 49184 | tf_op jit(solution)/shard_map/ppermute | solution.py:24
  22.6 5.9 %all-to-all-done = bf16[32,2,8192]{2,0,1:T(8,128)(2,1)S(1)} async-done(((bf16[32,2,8192]{2,0,1:T(8,128)(2,1)}), bf16[32,2,8192]{2,0,1:T(8,128)(2,1)S(1)}, u32[]{:S(2)}, u32[]{:S(2)}) %all-to-all-start) | async-done | bytes 1048608 | tf_op jit(solution)/shard_map/all_to_all | solution.py:272
  28.4 3.6 %all-to-all-start.1 = ((bf16[32,2,8192]{2,0,1:T(8,128)(2,1)}), bf16[32,2,8192]{2,0,1:T(8,128)(2,1)S(1)}, u32[]{:S(2)}, u32[]{:S(2)}) async-start(bf16[32,2,8192]{2,0,1:T(8,128)(2,1)} %bitcast.22), calls=%async_computation.1 | async-start | bytes 2097152 | tf_op jit(solution)/shard_map/all_to_all | solution.py:273
  32.3 0.5 copy-done.16
  32.8 1.3 multiply_convert_fusion.act_ref
  34.1 5.1 %fusion.7 = f32[64,512]{1,0:T(8,128)S(1)} fusion(bf16[64,8192]{1,0:T(8,128)(2,1)S(1)} %multiply_convert_fusion.act_ref, bf16[8192,512]{1,0:T(8,128)(2,1)} %param.17), kind=kOutput, calls=%fused_computation.19 | convolution fusion | flops 536870912 | bytes 9568256 | tf_op jit(solution)/shard_map/dot_general | solution.py:281
  39.7 2.1 %collective-permute-start.2 = (bf16[64,544]{1,0:T(8,128)(2,1)S(1)}, bf16[64,544]{1,0:T(8,128)(2,1)S(1)}, u32[]{:S(2)}, u32[]{:S(2)}) collective-permute-start(bf16[64,544]{1,0:T(8,128)(2,1)S(1)} %fusion.4), channel_id=1, source_target_pairs={{0,1},{1,0},{2,3},{3,2},{4,5},{5,4},{6,7},{7,6},{8,9},{9,8},{10,11... | collective-permute-start | bytes 208904 | tf_op jit(solution)/shard_map/ppermute | solution.py:288
  41.8 6.9 %collective-permute-done.2 = bf16[64,544]{1,0:T(8,128)(2,1)S(1)} collective-permute-done((bf16[64,544]{1,0:T(8,128)(2,1)S(1)}, bf16[64,544]{1,0:T(8,128)(2,1)S(1)}, u32[]{:S(2)}, u32[]{:S(2)}) %collective-permute-start.2) | collective-permute-done | bytes 69664 | tf_op jit(solution)/shard_map/ppermute | solution.py:288
  48.8 3.4 %copy-done.1 = bf16[512,8192]{1,0:T(8,128)(2,1)S(1)} copy-done((bf16[512,8192]{1,0:T(8,128)(2,1)S(1)}, bf16[512,8192]{1,0:T(8,128)(2,1)}, u32[]{:S(2)}) %copy-start.1) | copy-done | bytes 8388632
  52.2 0.8 copy-done.12
  52.9 11.3 %first_pass.1 = (f32[8,512,128]{2,1,0:T(8,128)S(1)}, bf16[16,80,128]{2,1,0:T(8,128)(2,1)S(1)}) custom-call(bf16[64,512]{1,0:T(8,128)(2,1)S(1)} %slice.85.low_ref, bf16[512,8192]{1,0:T(8,128)(2,1)S(1)} %copy-done.1, f32[1,8192]{1,0:T(1,128)S(1)} %bitcast.25, bf16[64,8192]{1,0:T(8,128)(2,1)S(1)} %multiply_convert_fusion.act_ref, ...), custom_call_target="tpu_custom_call" | custom-call | tf_op jit(solution)/shard_map/first_pass/pallas_call | solution.py:309
  64.3 1.3 copy-done.3
  65.7 21.0 %all-gather.5.cloned.1.call-done.v_ref = bf16[1024,512]{1,0:T(8,128)(2,1)} async-done(((bf16[64,512]{1,0:T(8,128)(2,1)}), bf16[1024,512]{1,0:T(8,128)(2,1)}) %all-gather.5.cloned.1.call-update) | async-done | bytes 1048592 | tf_op jit(solution)/shard_map/all_gather | solution.py:271
  86.7 1.2 copy-done.5
  87.9 1.2 copy-done.6
  89.2 1.0 copy-done.9
  90.2 19.3 %exchange.1 = (bf16[16,64,128]{2,1,0:T(8,128)(2,1)S(1)}, bf16[64,4096]{1,0:T(8,128)(2,1)S(1)}) custom-call(bf16[16,80,128]{2,1,0:T(8,128)(2,1)S(1)} %get-tuple-element.7.send_ref, f32[64,128]{1,0:T(8,128)S(1)} %reshape.14.rate_ref, bf16[64,4096]{1,0:T(8,128)(2,1)S(1)} %copy-done.9, bf16[1024,512]{1,0:T(8,128)(2,1)S(1)} %copy-done.5, ...), custom_call_target="tpu_custom_call" | custom-call | tf_op jit(solution)/shard_map/exchange/pallas_call | solution.py:334
  109.5 0.8 copy-done.7
  110.3 0.7 copy-done.10
  111.0 1.6 %copy-done.4 = f32[8,512,128]{2,1,0:T(8,128)S(1)} copy-done((f32[8,512,128]{2,1,0:T(8,128)S(1)}, f32[8,512,128]{2,1,0:T(8,128)}, u32[]{:S(2)}) %copy-start.4) | copy-done | bytes 2097176
  112.6 0.9 copy-done.11
  113.5 0.8 copy-done.13
  114.3 17.2 %second_pass.1 = bf16[32,16384]{1,0:T(8,128)(2,1)S(1)} custom-call(f32[8,512,128]{2,1,0:T(8,128)S(1)} %copy-done.4, bf16[64,8192]{1,0:T(8,128)(2,1)S(1)} %multiply_convert_fusion.act_ref, f32[64,32]{1,0:T(8,128)S(1)} %slice.57.terms_ref, f32[16,8192]{1,0:T(8,128)S(1)} %copy-done.2, bf16[16,64,128]{2,1,0:T(8,128)(2,1)S(1)} %copy-done.11, ...), custom_call_target="tpu_custom_call" | custom-call | tf_op jit(solution)/shard_map/second_pass/pallas_call | solution.py:351
  131.5 1.0 copy.27
  132.9 0.8 copy.28
  (38 shorter events, 1.4 us)
Async XLA Ops:
  7.2 32.1 %copy-start = (bf16[8192,32]{0,1:T(8,128)(2,1)S(1)}, bf16[8192,32]{0,1:T(8,128)(2,1)}, u32[]{:S(2)}) copy-start(bf16[8192,32]{0,1:T(8,128)(2,1)} %param.18) | copy-start | bytes 1572868
  7.2 58.5 %all-gather.3.cloned.1.call-start = ((), (), s32[]{:S(2)}) async-start(), calls=%async_computation.2 | async-start | bytes 1114112 | tf_op jit(solution)/shard_map/all_gather | solution.py:270
  7.9 9.1 %copy-start.15 = (f32[4,8192]{1,0:T(4,128)S(1)}, f32[4,8192]{1,0:T(4,128)}, u32[]{:S(2)}) copy-start(f32[4,8192]{1,0:T(4,128)} %param.15) | copy-start | bytes 393220
  7.9 9.2 %copy-start.14 = (bf16[32,16384]{1,0:T(8,128)(2,1)S(1)}, bf16[32,16384]{1,0:T(8,128)(2,1)}, u32[]{:S(2)}) copy-start(bf16[32,16384]{1,0:T(8,128)(2,1)} %param.14) | copy-start | bytes 3145732
  10.3 18.1 %all-to-all-start = ((bf16[32,2,8192]{2,0,1:T(8,128)(2,1)}), bf16[32,2,8192]{2,0,1:T(8,128)(2,1)S(1)}, u32[]{:S(2)}, u32[]{:S(2)}) async-start(bf16[32,2,8192]{2,0,1:T(8,128)(2,1)} %bitcast.23), calls=%async_computation | async-start | bytes 2097152 | tf_op jit(solution)/shard_map/all_to_all | solution.py:272
  13.9 72.8 %all-gather.5.cloned.1.call-start = ((), (), s32[]{:S(2)}) async-start(), calls=%async_computation.3 | async-start | bytes 1114112 | tf_op jit(solution)/shard_map/all_gather | solution.py:271
  15.0 7.6 %collective-permute-start = (bf16[3,8192]{1,0:T(4,128)(2,1)S(1)}, bf16[3,8192]{1,0:T(4,128)(2,1)S(1)}, u32[]{:S(2)}, u32[]{:S(2)}) collective-permute-start(bf16[3,8192]{1,0:T(4,128)(2,1)S(1)} %get-tuple-element.11), channel_id=1, source_target_pairs={{1,2},{3,4},{5,6},{7,8},{9,10},{11,12},{13,14},{15,16},{17,18},{19... | collective-permute-start | bytes 147464 | tf_op jit(solution)/shard_map/ppermute | solution.py:24
  16.3 6.3 %collective-permute-start.1 = (bf16[3,8192]{1,0:T(4,128)(2,1)S(1)}, bf16[3,8192]{1,0:T(4,128)(2,1)S(1)}, u32[]{:S(2)}, u32[]{:S(2)}) collective-permute-start(bf16[3,8192]{1,0:T(4,128)(2,1)S(1)} %get-tuple-element.10), channel_id=1, source_target_pairs={{1,3},{3,5},{5,7},{7,9},{9,11},{11,13},{13,15},{15,17},{17,19},{19... | collective-permute-start | bytes 147464 | tf_op jit(solution)/shard_map/ppermute | solution.py:24
  28.4 82.5 %all-to-all-start.1 = ((bf16[32,2,8192]{2,0,1:T(8,128)(2,1)}), bf16[32,2,8192]{2,0,1:T(8,128)(2,1)S(1)}, u32[]{:S(2)}, u32[]{:S(2)}) async-start(bf16[32,2,8192]{2,0,1:T(8,128)(2,1)} %bitcast.22), calls=%async_computation.1 | async-start | bytes 2097152 | tf_op jit(solution)/shard_map/all_to_all | solution.py:273
  32.0 0.8 copy-start.16
  34.1 7.7 %copy-start.2 = (f32[16,8192]{1,0:T(8,128)S(1)}, f32[16,8192]{1,0:T(8,128)}, u32[]{:S(2)}) copy-start(f32[16,8192]{1,0:T(8,128)} %decay_ref.3) | copy-start | bytes 1572868
  39.7 9.0 %collective-permute-start.2 = (bf16[64,544]{1,0:T(8,128)(2,1)S(1)}, bf16[64,544]{1,0:T(8,128)(2,1)S(1)}, u32[]{:S(2)}, u32[]{:S(2)}) collective-permute-start(bf16[64,544]{1,0:T(8,128)(2,1)S(1)} %fusion.4), channel_id=1, source_target_pairs={{0,1},{1,0},{2,3},{3,2},{4,5},{5,4},{6,7},{7,6},{8,9},{9,8},{10,11... | collective-permute-start | bytes 208904 | tf_op jit(solution)/shard_map/ppermute | solution.py:288
  48.8 3.4 %copy-start.1 = (bf16[512,8192]{1,0:T(8,128)(2,1)S(1)}, bf16[512,8192]{1,0:T(8,128)(2,1)}, u32[]{:S(2)}) copy-start(bf16[512,8192]{1,0:T(8,128)(2,1)} %up_ref.1) | copy-start | bytes 25165828
  52.2 0.8 copy-start.12
  64.3 1.4 copy-start.3
  86.7 1.2 copy-start.5
  87.9 1.2 copy-start.6
  89.1 1.0 copy-start.9
  109.5 0.8 copy-start.7
  110.3 0.7 copy-start.10
  111.0 1.6 %copy-start.4 = (f32[8,512,128]{2,1,0:T(8,128)S(1)}, f32[8,512,128]{2,1,0:T(8,128)}, u32[]{:S(2)}) copy-start(f32[8,512,128]{2,1,0:T(8,128)} %copy-done.3) | copy-start | bytes 6291460
  112.6 0.9 copy-start.11
  113.5 0.8 copy-start.13
  131.5 1.4 copy-start.8
Sparse Core Ops, SparseCore 0:
  10.2 37.3 all-gather.2
  49.7 36.9 all-gather.4

commit v3 on v2

--- a/solution.py
+++ b/solution.py
@@ -178,27 +178,61 @@
             keep(i).wait()
 
 
-def exchange(n_ctx, rows_state, rows_total, send_ref, rate_ref, q_ref, k_ref, v_ref,
-             back_ref, mixed_ref, got, reply, send_sem, got_sem, reply_sem, back_sem):
+def swap_copies(n_ch, src_ref, dst_ref, keep_sem, send_sem, recv_sem):
+    me = lax.axis_index("ch")
+    width = dst_ref.shape[2]
+    mine = pl.ds(pl.multiple_of(me * width, width), width)
+    copies = []
+    for k in range(1, n_ch):
+        peer = lax.rem(me + k, n_ch)
+        theirs = pl.ds(pl.multiple_of(peer * width, width), width)
+        copies.append(pltpu.make_async_remote_copy(
+            src_ref=src_ref.at[:, theirs], dst_ref=dst_ref.at[me], send_sem=send_sem.at[k],
+            recv_sem=recv_sem.at[k], device_id={"ch": peer}, device_id_type=MESH))
+    copies.append(pltpu.make_async_copy(src_ref.at[:, mine], dst_ref.at[me], keep_sem))
+    return copies
+
+
+def greet(axis, size):
+    me = lax.axis_index(axis)
+    for k in range(1, size):
+        peer = lax.rem(me + k, size)
+        pl.semaphore_signal(
+            pltpu.get_barrier_semaphore(), inc=1, device_id={axis: peer}, device_id_type=MESH)
+
+
+def swap_input(n_ch, src_ref, dst_ref, keep_sem, send_sem, recv_sem):
+    greet("ch", n_ch)
+    pl.semaphore_wait(pltpu.get_barrier_semaphore(), n_ch - 1)
+    copies = swap_copies(n_ch, src_ref, dst_ref, keep_sem, send_sem, recv_sem)
+    for copy in copies:
+        copy.start()
+    for copy in copies:
+        copy.wait()
+
+
+def exchange(n_ctx, n_ch, rows_state, rows_total, send_ref, rate_ref, q_ref, kv_ref, gate_ref,
+             back_ref, mixed_ref, gate_out, got, reply, send_sem, got_sem, reply_sem, back_sem,
+             keep_sem, gate_send, gate_recv):
     me = lax.axis_index("ctx")
     rows = q_ref.shape[0]
-    groups = k_ref.shape[1] // HEAD_DIM
+    groups = kv_ref.shape[1] // 2 // HEAD_DIM
     block = q_ref.shape[1] // groups
 
     def attend(g, carry):
-        at = pl.ds(pl.multiple_of(g * HEAD_DIM, HEAD_DIM), HEAD_DIM)
+        k_at = pl.ds(pl.multiple_of(g * HEAD_DIM, HEAD_DIM), HEAD_DIM)
+        v_at = pl.ds(pl.multiple_of((groups + g) * HEAD_DIM, HEAD_DIM), HEAD_DIM)
         first = pl.multiple_of(g * block, HEAD_DIM)
         parts = attend_group(
-            me * rows, rows, q_ref[:, pl.ds(first, block)], k_ref[:, at], v_ref[:, at])
+            me * rows, rows, q_ref[:, pl.ds(first, block)], kv_ref[:, k_at], kv_ref[:, v_at])
         for h, part in enumerate(parts):
             mixed_ref[:, pl.ds(pl.multiple_of(first + h * HEAD_DIM, HEAD_DIM), HEAD_DIM)] = part
         return carry
 
-    barrier = pltpu.get_barrier_semaphore()
-    for k in range(1, n_ctx):
-        peer = lax.rem(me + k, n_ctx)
-        pl.semaphore_signal(barrier, inc=1, device_id={"ctx": peer}, device_id_type=MESH)
-    pl.semaphore_wait(barrier, n_ctx - 1)
+    greet("ctx", n_ctx)
+    greet("ch", n_ch)
+    pl.semaphore_wait(pltpu.get_barrier_semaphore(), n_ctx + n_ch - 2)
+    gates = swap_copies(n_ch, gate_ref, gate_out, keep_sem, gate_send, gate_recv)
 
     def there(k):
         peer = lax.rem(me + k, n_ctx)
@@ -214,6 +248,8 @@
 
     for k in range(1, n_ctx):
         there(k).start()
+    for copy in gates:
+        copy.start()
     got[me] = send_ref[me]
     half = (groups + 1) // 2
     lax.fori_loop(0, half, attend, 0)
@@ -242,6 +278,8 @@
     lax.fori_loop(half, groups, attend, 0)
     for k in range(1, n_ctx):
         back(k).wait()
+    for copy in gates:
+        copy.wait()
 
 
 def attend_group(query_first, rows, q, k, v):
@@ -267,11 +305,24 @@
     decay_rate, skip_gain, queries, key_rows, value_rows,
 ):
     n_ctx, n_ch = lax.axis_size("ctx"), lax.axis_size("ch")
-    keys = lax.all_gather(key_rows, "ctx", axis=0, tiled=True)
-    values = lax.all_gather(value_rows, "ctx", axis=0, tiled=True)
-    inner_in = lax.all_to_all(mamba_input, "ch", split_axis=1, concat_axis=0, tiled=True)
-    inner_gate = lax.all_to_all(mamba_gate, "ch", split_axis=1, concat_axis=0, tiled=True)
-    rows, channels = inner_in.shape
+    kv = lax.all_gather(
+        jnp.concatenate([key_rows, value_rows], axis=1), "ctx", axis=0, tiled=True)
+    here, channels = mamba_input.shape[0], mamba_input.shape[1] // n_ch
+    rows = here * n_ch
+    limit = 56 * 1024 * 1024
+    hbm = pl.BlockSpec(memory_space=pl.ANY)
+    swapped = jax.ShapeDtypeStruct((n_ch, here, channels), jnp.bfloat16)
+    swap_sems = [pltpu.SemaphoreType.DMA, pltpu.SemaphoreType.DMA((n_ch,)),
+                 pltpu.SemaphoreType.DMA((n_ch,))]
+    inner_in = pl.pallas_call(
+        functools.partial(swap_input, n_ch),
+        in_specs=[hbm],
+        out_specs=hbm,
+        out_shape=swapped,
+        scratch_shapes=swap_sems,
+        compiler_params=pltpu.CompilerParams(collective_id=2, has_side_effects=True),
+        name="swap_input",
+    )(mamba_input).reshape(rows, channels)
     rim_rows = halo(mamba_input, n_ctx, n_ch)
     padded = jnp.concatenate([rim_rows, inner_in], axis=0).astype(jnp.float32)
     conv_sum = conv_bias[None, :] + sum(
@@ -295,7 +346,6 @@
     whole = lambda shape: pl.BlockSpec(shape, lambda i: (0,) * len(shape))
     cols = lambda r: pl.BlockSpec((r, TILE), lambda i: (0, i))
     step_spec = pl.BlockSpec((1, rows * SUBS, LANES), lambda i: (i, 0, 0))
-    limit = 32 * 1024 * 1024
     tile_rows = rows * SUBS
     splits = max(1, n_ctx * LANES // channels)
     groups, held = n_ctx // splits, STATE // splits
@@ -331,22 +381,23 @@
         decay_rate, (me % splits * held, me // splits * chunk), (held, chunk))
     my_rate = (my_rate * (-LOG2E)).reshape(rows_state, LANES)
     vmem = pl.BlockSpec(memory_space=pltpu.VMEM)
-    incoming, attention_out = pl.pallas_call(
-        functools.partial(exchange, n_ctx, rows_state, subs),
-        in_specs=[vmem] * 5,
-        out_specs=[vmem] * 2,
+    incoming, attention_out, inner_gate = pl.pallas_call(
+        functools.partial(exchange, n_ctx, n_ch, rows_state, subs),
+        in_specs=[vmem] * 4 + [hbm],
+        out_specs=[vmem] * 2 + [hbm],
         out_shape=[
             jax.ShapeDtypeStruct((n_ctx, rows_back, LANES), bf16),
             jax.ShapeDtypeStruct(queries.shape, bf16),
+            swapped,
         ],
         scratch_shapes=[
             pltpu.VMEM((n_ctx, rows_all, LANES), bf16),
             pltpu.VMEM((n_ctx, rows_back, LANES), bf16),
-        ] + [pltpu.SemaphoreType.DMA((n_ctx,))] * 4,
+        ] + [pltpu.SemaphoreType.DMA((n_ctx,))] * 4 + swap_sems,
         compiler_params=pltpu.CompilerParams(
             collective_id=0, has_side_effects=True, vmem_limit_bytes=limit),
         name="exchange",
-    )(packed, my_rate, queries, keys, values)
+    )(packed, my_rate, queries, kv, mamba_gate)
 
     mamba_out = pl.pallas_call(
         functools.partial(second_pass, packing, n_ch),
@@ -373,7 +424,8 @@
         compiler_params=pltpu.CompilerParams(
             collective_id=1, has_side_effects=True, vmem_limit_bytes=limit),
         name="second_pass",
-    )(step_rows, activation, state_terms, decay_rate, incoming, inner_gate, skip_gain[None])
+    )(step_rows, activation, state_terms, decay_rate, incoming,
+      inner_gate.reshape(rows, channels), skip_gain[None])
     return (mamba_out, attention_out)
 
 

time: 142 us -> 117 us (0.82)
  the two profiles are of different devices: /device:TPU:16 before, /device:TPU:0 now
where the time goes in v3:
time: 117 us; the launch traced here: 116 us
  Pallas kernels  79.1 us (68%)
  between operations  14.2 us (12%)
  local copies, waits for them, and re-layouts  7.43 us (6%)
  matrix products  5.62 us (5%)
  other arithmetic  5.22 us (4%)
  waiting for transfers between devices  3.08 us (3%)
  starting transfers between devices  1.44 us (1%)
    pallas_call x1, Pallas kernels, local(): pl.pallas_call(functools.partial(swap_input, n_ch), in_specs=[hbm], out_s...  24.1 us
    pallas_call x1, Pallas kernels, local(): pl.pallas_call(functools.partial(exchange, n_ctx, n_ch, rows_state, subs)...  24.1 us
    pallas_call x1, Pallas kernels, local(): pl.pallas_call(functools.partial(second_pass, packing, n_ch), grid=(tiles...  18.1 us
    pallas_call x1, Pallas kernels, local(): pl.pallas_call(functools.partial(first_pass, packing), grid=(tiles,), in_...  12.9 us
    dot_general x1, matrix products, local(): jnp.dot(activation, step_down, preferred_element_type=jnp.float32)  5.19 us
    unnamed x10, local copies, waits for them, and re-layouts  3.14 us
    ppermute x1, waiting for transfers between devices, local(): summed = summed + lax.ppermute(part_b, 'ch', pairs).astype(jnp.float32)  3.05 us
  transfers between devices with their start and end apart: 4, of which 1 were waited for; matrix products, arithmetic and copies ran while one was open for 12% of the time, Pallas kernels for 32%

profile of v3, /device:TPU:0, one launch (start us, length us, event | category | flops | bytes accessed | tf_op | source)
XLA Modules:
  0.0 116.1 jit_solution(17428440484986377769)
XLA Ops:
  7.2 0.0 copy-start
  7.2 0.0 all-gather.2.cloned.1.call-start
  7.2 1.1 fusion.5
  8.3 0.7 collective-permute-start
  9.0 0.7 collective-permute-start.1
  9.7 1.5 %pad_maximum_fusion.1 = bf16[64,1024]{1,0:T(8,128)(2,1)} fusion(bf16[64,512]{1,0:T(8,128)(2,1)} %param.25, bf16[64,512]{1,0:T(8,128)(2,1)} %param.24), kind=kLoop, calls=%fused_computation.14 | loop fusion | flops 262144 | bytes 262144 | tf_op jit(solution)/shard_map/concatenate | solution.py:309
  11.2 0.0 all-gather.2.cloned.1.call-update
  11.2 1.4 %fusion.6 = (f32[1,8192]{1,0:T(1,128)S(1)}, f32[1,8192]{1,0:T(1,128)S(1)}, f32[1,8192]{1,0:T(1,128)S(1)}, f32[1,8192]{1,0:T(1,128)S(1)}) fusion(f32[4,8192]{1,0:T(4,128)} %param.15), kind=kLoop, calls=%fused_computation.17 | loop fusion | bytes 262144 | tf_op jit(solution)/shard_map/slice | solution.py:329
  12.6 24.1 %swap_input.1 = bf16[2,32,8192]{2,1,0:T(8,128)(2,1)} custom-call(bf16[32,16384]{1,0:T(8,128)(2,1)} %src_ref.1), custom_call_target="tpu_custom_call" | custom-call | tf_op jit(solution)/shard_map/swap_input/pallas_call | solution.py:317
  36.7 0.0 copy-start.3
  36.7 0.0 collective-permute-done
  36.7 0.0 collective-permute-done.1
  36.8 1.5 %maximum_convert_fusion = f32[67,8192]{1,0:T(8,128)S(1)} fusion(bf16[64,8192]{1,0:T(8,128)(2,1)} %bitcast.12, bf16[3,8192]{1,0:T(4,128)(2,1)S(1)} %add.35), kind=kLoop, calls=%fused_computation.9 | loop fusion | flops 2195456 | bytes 3293184 | tf_op jit(solution)/shard_map/convert_element_type | solution.py:327
  38.3 0.0 copy-done.3
  38.3 1.3 %multiply_convert_fusion.act_ref = bf16[64,8192]{1,0:T(8,128)(2,1)S(1)} fusion(f32[67,8192]{1,0:T(8,128)S(1)} %maximum_convert_fusion, f32[8192]{0:T(1024)S(1)} %bitcast.16, f32[8192]{0:T(1024)S(1)} %bitcast.17, f32[8192]{0:T(1024)S(1)} %bitcast.15, f32[8192]{0:T(1024)S(1)} %bitcast.14, f32[8192]{0:T(1024)S(1)} %copy-done.3), kind=kLoop, calls=%fused_computation.8 | loop fusion | flops 6815744 | bytes 9601024 | tf_op jit(solution)/shard_map/convert_element_type | solution.py:331
  39.6 0.0 copy-done
  39.6 0.0 copy-start.1
  39.7 0.4 fusion.8
  40.1 5.2 %fusion.7 = f32[64,512]{1,0:T(8,128)S(1)} fusion(bf16[64,8192]{1,0:T(8,128)(2,1)S(1)} %multiply_convert_fusion.act_ref, bf16[8192,512]{1,0:T(8,128)(2,1)} %param.17), kind=kOutput, calls=%fused_computation.18 | convolution fusion | flops 536870912 | bytes 9568256 | tf_op jit(solution)/shard_map/dot_general | solution.py:332
  45.3 0.0 copy-done.1
  45.3 0.1 collective-permute-start.2
  45.4 0.8 dynamic-slice_multiply_fusion
  46.2 0.6 reshape.15.rate_ref
  46.8 3.1 %collective-permute-done.2 = bf16[64,544]{1,0:T(8,128)(2,1)S(1)} collective-permute-done((bf16[64,544]{1,0:T(8,128)(2,1)S(1)}, bf16[64,544]{1,0:T(8,128)(2,1)S(1)}, u32[]{:S(2)}, u32[]{:S(2)}) %collective-permute-start.2) | collective-permute-done | bytes 69664 | tf_op jit(solution)/shard_map/ppermute | solution.py:339
  49.9 0.6 slice.85.low_ref
  50.5 0.6 slice.57.terms_ref
  51.1 12.9 %first_pass.1 = (f32[8,512,128]{2,1,0:T(8,128)}, bf16[16,80,128]{2,1,0:T(8,128)(2,1)}) custom-call(bf16[64,512]{1,0:T(8,128)(2,1)} %slice.85.low_ref, bf16[512,8192]{1,0:T(8,128)(2,1)} %up_ref.1, f32[1,8192]{1,0:T(1,128)} %bitcast.18, bf16[64,8192]{1,0:T(8,128)(2,1)} %copy-done.1, f32[64,32]{1,0:T(8,128)} %slice.57.terms_ref, f32[16,8192]{1,0:T(8,128)} %decay_ref.3), custom_call_target="tpu_custom_call" | custom-call | tf_op jit(solution)/shard_map/first_pass/pallas_call | solution.py:359
  63.9 24.1 %exchange.1 = (bf16[16,64,128]{2,1,0:T(8,128)(2,1)}, bf16[64,4096]{1,0:T(8,128)(2,1)}, bf16[2,32,8192]{2,1,0:T(8,128)(2,1)}) custom-call(bf16[16,80,128]{2,1,0:T(8,128)(2,1)} %get-tuple-element.8.send_ref, f32[64,128]{1,0:T(8,128)} %reshape.15.rate_ref, bf16[64,4096]{1,0:T(8,128)(2,1)} %q_ref.1, bf16[1024,1024]{1,0:T(8,128)(2,1)} %all-gather.2.cloned.1.call-done.kv_ref, ...), custom_call_target="tpu_custom_call" | custom-call | tf_op jit(solution)/shard_map/exchange/pallas_call | solution.py:384
  88.0 18.1 %second_pass.1 = bf16[32,16384]{1,0:T(8,128)(2,1)} custom-call(f32[8,512,128]{2,1,0:T(8,128)} %get-tuple-element.7.step_ref, bf16[64,8192]{1,0:T(8,128)(2,1)} %copy-done.1, f32[64,32]{1,0:T(8,128)} %slice.57.terms_ref, f32[16,8192]{1,0:T(8,128)} %decay_ref.3, bf16[16,64,128]{2,1,0:T(8,128)(2,1)} %get-tuple-element.9.incoming_ref, bf16[64,8192]{1,0:T(8,128)(2,1)} %bitcast.13, ...), custom_call_target="tpu_custom_call" | custom-call | tf_op jit(solution)/shard_map/second_pass/pallas_call | solution.py:402
  106.1 0.0 copy-start.2
  106.1 2.3 %copy.19 = bf16[32,16384]{1,0:T(8,128)(2,1)} copy(bf16[32,16384]{1,0:T(8,128)(2,1)} %second_pass.1) | data formatting | bytes 2097152
  108.5 0.8 copy.20
  (5 shorter events, 0.1 us)
Async XLA Ops:
  7.2 32.5 %copy-start = (bf16[8192,32]{0,1:T(8,128)(2,1)S(1)}, bf16[8192,32]{0,1:T(8,128)(2,1)}, u32[]{:S(2)}) copy-start(bf16[8192,32]{0,1:T(8,128)(2,1)} %param.18) | copy-start | bytes 1572868
  7.2 56.8 %all-gather.2.cloned.1.call-start = ((), (), s32[]{:S(2)}) async-start(), calls=%async_computation | async-start | bytes 2228224 | tf_op jit(solution)/shard_map/all_gather | solution.py:308
  8.3 28.4 %collective-permute-start = (bf16[3,8192]{1,0:T(4,128)(2,1)S(1)}, bf16[3,8192]{1,0:T(4,128)(2,1)S(1)}, u32[]{:S(2)}, u32[]{:S(2)}) collective-permute-start(bf16[3,8192]{1,0:T(4,128)(2,1)S(1)} %get-tuple-element.13), channel_id=1, source_target_pairs={{1,2},{3,4},{5,6},{7,8},{9,10},{11,12},{13,14},{15,16},{17,18},{19... | collective-permute-start | bytes 147464 | tf_op jit(solution)/shard_map/ppermute | solution.py:24
  9.0 27.7 %collective-permute-start.1 = (bf16[3,8192]{1,0:T(4,128)(2,1)S(1)}, bf16[3,8192]{1,0:T(4,128)(2,1)S(1)}, u32[]{:S(2)}, u32[]{:S(2)}) collective-permute-start(bf16[3,8192]{1,0:T(4,128)(2,1)S(1)} %get-tuple-element.12), channel_id=1, source_target_pairs={{1,3},{3,5},{5,7},{7,9},{9,11},{11,13},{13,15},{15,17},{17,19},{19... | collective-permute-start | bytes 147464 | tf_op jit(solution)/shard_map/ppermute | solution.py:24
  36.7 1.6 %copy-start.3 = (f32[8192]{0:T(1024)S(1)}, f32[8192]{0:T(1024)}, u32[]{:S(2)}) copy-start(f32[8192]{0:T(1024)} %param.16) | copy-start | bytes 98308
  39.6 5.7 %copy-start.1 = (bf16[64,8192]{1,0:T(8,128)(2,1)}, bf16[64,8192]{1,0:T(8,128)(2,1)S(1)}, u32[]{:S(2)}) copy-start(bf16[64,8192]{1,0:T(8,128)(2,1)S(1)} %multiply_convert_fusion.act_ref) | copy-start | bytes 3145732
  45.3 4.5 %collective-permute-start.2 = (bf16[64,544]{1,0:T(8,128)(2,1)S(1)}, bf16[64,544]{1,0:T(8,128)(2,1)S(1)}, u32[]{:S(2)}, u32[]{:S(2)}) collective-permute-start(bf16[64,544]{1,0:T(8,128)(2,1)S(1)} %fusion.4), channel_id=1, source_target_pairs={{0,1},{1,0},{2,3},{3,2},{4,5},{5,4},{6,7},{7,6},{8,9},{9,8},{10,11... | collective-permute-start | bytes 208904 | tf_op jit(solution)/shard_map/ppermute | solution.py:339
  106.1 2.3 %copy-start.2 = (bf16[64,4096]{1,0:T(8,128)(2,1)S(1)}, bf16[64,4096]{1,0:T(8,128)(2,1)}, u32[]{:S(2)}) copy-start(bf16[64,4096]{1,0:T(8,128)(2,1)} %get-tuple-element.21) | copy-start | bytes 1572868
Sparse Core Ops, SparseCore 0:
  11.3 47.0 all-gather.1

commit v4 on v3

--- a/solution.py
+++ b/solution.py
@@ -51,9 +51,48 @@
     return spread_ref[pl.ds(index, SUBS, stride=0), :]
 
 
-def first_pass(packing, low_ref, up_ref, bias_ref, act_ref, terms_ref, decay_ref,
-               step_ref, packed_ref, spread, act_rows, rates, pack):
+PIECES = 4
+
+
+def swap_copies(n_ch, src_ref, dst_ref, keep_sem, send_sem, recv_sem):
+    me = lax.axis_index("ch")
+    width = dst_ref.shape[2]
+    piece = width // PIECES
+    copies = []
+    for p in range(PIECES):
+        target = pl.ds(p * piece, piece)
+        for k in range(1, n_ch):
+            peer = lax.rem(me + k, n_ch)
+            source = pl.ds(pl.multiple_of(peer * width + p * piece, LANES), piece)
+            copies.append(pltpu.make_async_remote_copy(
+                src_ref=src_ref.at[:, source], dst_ref=dst_ref.at[me, :, target],
+                send_sem=send_sem.at[p, k], recv_sem=recv_sem.at[p, k],
+                device_id={"ch": peer}, device_id_type=MESH))
+    mine = pl.ds(pl.multiple_of(me * width, LANES), width)
+    copies.append(pltpu.make_async_copy(src_ref.at[:, mine], dst_ref.at[me], keep_sem))
+    return copies
+
+
+def greet(axis, size):
+    me = lax.axis_index(axis)
+    for k in range(1, size):
+        peer = lax.rem(me + k, size)
+        pl.semaphore_signal(
+            pltpu.get_barrier_semaphore(), inc=1, device_id={axis: peer}, device_id_type=MESH)
+
+
+def first_pass(packing, n_ch, low_ref, up_ref, bias_ref, act_ref, terms_ref, decay_ref, gate_ref,
+               step_ref, packed_ref, gate_out, spread, act_rows, rates, pack,
+               keep_sem, send_sem, recv_sem):
     rows = act_ref.shape[0]
+    gates = swap_copies(n_ch, gate_ref, gate_out, keep_sem, send_sem, recv_sem)
+
+    @pl.when(pl.program_id(0) == 0)
+    def _():
+        greet("ch", n_ch)
+        pl.semaphore_wait(pltpu.get_barrier_semaphore(), n_ch - 1)
+        for copy in gates:
+            copy.start()
 
     @pl.when(pl.program_id(0) == 0)
     def _():
@@ -77,7 +116,7 @@
         return states, total + step
 
     zero = jnp.zeros((SUBS, LANES), jnp.float32)
-    states, total = lax.fori_loop(0, rows, token, ((zero,) * STATE, zero), unroll=4)
+    states, total = lax.fori_loop(0, rows, token, ((zero,) * STATE, zero), unroll=8)
     splits, subs, held, rows_state = packing
     total_hi = total.astype(jnp.bfloat16).astype(jnp.float32)
     pack[...] = jnp.zeros_like(pack)
@@ -88,6 +127,11 @@
         pack[part, rows_state : rows_state + subs] = total_hi[cut]
         pack[part, rows_state + subs : rows_state + 2 * subs] = (total - total_hi)[cut]
     packed_ref[...] = pack[...].astype(jnp.bfloat16)
+
+    @pl.when(pl.program_id(0) == pl.num_programs(0) - 1)
+    def _():
+        for copy in gates:
+            copy.wait()
 
 
 def second_pass(packing, n_ch, step_ref, act_ref, terms_ref, decay_ref, incoming_ref, gate_ref, skip_ref,
@@ -135,7 +179,7 @@
             row = (part % splits * held + n) * SUBS + part // splits * subs
             entering[row : row + subs, :] = wide[part, n * subs : (n + 1) * subs]
     start = tuple(entering[n * SUBS : (n + 1) * SUBS, :] for n in range(STATE))
-    lax.fori_loop(0, rows, token, start, unroll=4)
+    lax.fori_loop(0, rows, token, start, unroll=8)
     first = pl.multiple_of(tile * TILE, TILE)
     for sub in range(SUBS):
         cols = slice(sub * LANES, (sub + 1) * LANES)
@@ -178,29 +222,6 @@
             keep(i).wait()
 
 
-def swap_copies(n_ch, src_ref, dst_ref, keep_sem, send_sem, recv_sem):
-    me = lax.axis_index("ch")
-    width = dst_ref.shape[2]
-    mine = pl.ds(pl.multiple_of(me * width, width), width)
-    copies = []
-    for k in range(1, n_ch):
-        peer = lax.rem(me + k, n_ch)
-        theirs = pl.ds(pl.multiple_of(peer * width, width), width)
-        copies.append(pltpu.make_async_remote_copy(
-            src_ref=src_ref.at[:, theirs], dst_ref=dst_ref.at[me], send_sem=send_sem.at[k],
-            recv_sem=recv_sem.at[k], device_id={"ch": peer}, device_id_type=MESH))
-    copies.append(pltpu.make_async_copy(src_ref.at[:, mine], dst_ref.at[me], keep_sem))
-    return copies
-
-
-def greet(axis, size):
-    me = lax.axis_index(axis)
-    for k in range(1, size):
-        peer = lax.rem(me + k, size)
-        pl.semaphore_signal(
-            pltpu.get_barrier_semaphore(), inc=1, device_id={axis: peer}, device_id_type=MESH)
-
-
 def swap_input(n_ch, src_ref, dst_ref, keep_sem, send_sem, recv_sem):
     greet("ch", n_ch)
     pl.semaphore_wait(pltpu.get_barrier_semaphore(), n_ch - 1)
@@ -211,9 +232,8 @@
         copy.wait()
 
 
-def exchange(n_ctx, n_ch, rows_state, rows_total, send_ref, rate_ref, q_ref, kv_ref, gate_ref,
-             back_ref, mixed_ref, gate_out, got, reply, send_sem, got_sem, reply_sem, back_sem,
-             keep_sem, gate_send, gate_recv):
+def exchange(n_ctx, rows_state, rows_total, send_ref, rate_ref, q_ref, kv_ref,
+             back_ref, mixed_ref, got, reply, send_sem, got_sem, reply_sem, back_sem):
     me = lax.axis_index("ctx")
     rows = q_ref.shape[0]
     groups = kv_ref.shape[1] // 2 // HEAD_DIM
@@ -230,9 +250,7 @@
         return carry
 
     greet("ctx", n_ctx)
-    greet("ch", n_ch)
-    pl.semaphore_wait(pltpu.get_barrier_semaphore(), n_ctx + n_ch - 2)
-    gates = swap_copies(n_ch, gate_ref, gate_out, keep_sem, gate_send, gate_recv)
+    pl.semaphore_wait(pltpu.get_barrier_semaphore(), n_ctx - 1)
 
     def there(k):
         peer = lax.rem(me + k, n_ctx)
@@ -248,8 +266,6 @@
 
     for k in range(1, n_ctx):
         there(k).start()
-    for copy in gates:
-        copy.start()
     got[me] = send_ref[me]
     half = (groups + 1) // 2
     lax.fori_loop(0, half, attend, 0)
@@ -278,8 +294,6 @@
     lax.fori_loop(half, groups, attend, 0)
     for k in range(1, n_ctx):
         back(k).wait()
-    for copy in gates:
-        copy.wait()
 
 
 def attend_group(query_first, rows, q, k, v):
@@ -312,8 +326,8 @@
     limit = 56 * 1024 * 1024
     hbm = pl.BlockSpec(memory_space=pl.ANY)
     swapped = jax.ShapeDtypeStruct((n_ch, here, channels), jnp.bfloat16)
-    swap_sems = [pltpu.SemaphoreType.DMA, pltpu.SemaphoreType.DMA((n_ch,)),
-                 pltpu.SemaphoreType.DMA((n_ch,))]
+    swap_sems = [pltpu.SemaphoreType.DMA, pltpu.SemaphoreType.DMA((PIECES, n_ch)),
+                 pltpu.SemaphoreType.DMA((PIECES, n_ch))]
     inner_in = pl.pallas_call(
         functools.partial(swap_input, n_ch),
         in_specs=[hbm],
@@ -356,48 +370,49 @@
     rows_back = -(-rows_state // 16) * 16
     rows_all = -(-(rows_state + 2 * subs) // 16) * 16
     packing = (splits, subs, held, rows_state)
-    step_rows, packed = pl.pallas_call(
-        functools.partial(first_pass, packing),
+    step_rows, packed, inner_gate = pl.pallas_call(
+        functools.partial(first_pass, packing, n_ch),
         grid=(tiles,),
         in_specs=[whole((rows, rank)), cols(rank), cols(1), cols(rows), whole((rows, 2 * STATE)),
-                  cols(STATE)],
-        out_specs=[step_spec, pl.BlockSpec((parts, rows_all, LANES), lambda i: (i, 0, 0))],
+                  cols(STATE), hbm],
+        out_specs=[step_spec, pl.BlockSpec((parts, rows_all, LANES), lambda i: (i, 0, 0)), hbm],
         out_shape=[
             jax.ShapeDtypeStruct((tiles, tile_rows, LANES), f32),
             jax.ShapeDtypeStruct((n_ctx, rows_all, LANES), bf16),
+            swapped,
         ],
         scratch_shapes=[
             pltpu.VMEM((STATE * rows, LANES), f32),
             pltpu.VMEM((tile_rows, LANES), f32),
             pltpu.VMEM((STATE * SUBS, LANES), f32),
             pltpu.VMEM((parts, rows_all, LANES), f32),
-        ],
-        compiler_params=pltpu.CompilerParams(vmem_limit_bytes=limit),
+        ] + swap_sems,
+        compiler_params=pltpu.CompilerParams(
+            collective_id=3, has_side_effects=True, vmem_limit_bytes=limit),
         name="first_pass",
-    )(step_low, step_up, step_bias[None], activation, state_terms, decay_rate)
+    )(step_low, step_up, step_bias[None], activation, state_terms, decay_rate, mamba_gate)
 
     me = lax.axis_index("ctx")
     my_rate = lax.dynamic_slice(
         decay_rate, (me % splits * held, me // splits * chunk), (held, chunk))
     my_rate = (my_rate * (-LOG2E)).reshape(rows_state, LANES)
     vmem = pl.BlockSpec(memory_space=pltpu.VMEM)
-    incoming, attention_out, inner_gate = pl.pallas_call(
-        functools.partial(exchange, n_ctx, n_ch, rows_state, subs),
-        in_specs=[vmem] * 4 + [hbm],
-        out_specs=[vmem] * 2 + [hbm],
+    incoming, attention_out = pl.pallas_call(
+        functools.partial(exchange, n_ctx, rows_state, subs),
+        in_specs=[vmem] * 4,
+        out_specs=[vmem] * 2,
         out_shape=[
             jax.ShapeDtypeStruct((n_ctx, rows_back, LANES), bf16),
             jax.ShapeDtypeStruct(queries.shape, bf16),
-            swapped,
         ],
         scratch_shapes=[
             pltpu.VMEM((n_ctx, rows_all, LANES), bf16),
             pltpu.VMEM((n_ctx, rows_back, LANES), bf16),
-        ] + [pltpu.SemaphoreType.DMA((n_ctx,))] * 4 + swap_sems,
+        ] + [pltpu.SemaphoreType.DMA((n_ctx,))] * 4,
         compiler_params=pltpu.CompilerParams(
             collective_id=0, has_side_effects=True, vmem_limit_bytes=limit),
         name="exchange",
-    )(packed, my_rate, queries, kv, mamba_gate)
+    )(packed, my_rate, queries, kv)
 
     mamba_out = pl.pallas_call(
         functools.partial(second_pass, packing, n_ch),

time: 117 us -> 118 us (level)
  the two profiles are of different devices: /device:TPU:0 before, /device:TPU:16 now
where the time goes in v4:
time: 118 us; the launch traced here: 117 us
  Pallas kernels  78.5 us (67%)
  between operations  14.2 us (12%)
  local copies, waits for them, and re-layouts  7.38 us (6%)
  matrix products  5.51 us (5%)
  other arithmetic  5.27 us (4%)
  waiting for transfers between devices  3.6 us (3%)
  starting transfers between devices  2.22 us (2%)
    pallas_call x1, Pallas kernels, local(): pl.pallas_call(functools.partial(exchange, n_ctx, rows_state, subs), in_s...  22.1 us
    pallas_call x1, Pallas kernels, local(): pl.pallas_call(functools.partial(swap_input, n_ch), in_specs=[hbm], out_s...  19.9 us
    pallas_call x1, Pallas kernels, local(): pl.pallas_call(functools.partial(first_pass, packing, n_ch), grid=(tiles,...  19.1 us
    pallas_call x1, Pallas kernels, local(): pl.pallas_call(functools.partial(second_pass, packing, n_ch), grid=(tiles...  17.4 us
    dot_general x1, matrix products, local(): jnp.dot(activation, step_down, preferred_element_type=jnp.float32)  5.08 us
    ppermute x1, waiting for transfers between devices, local(): summed = summed + lax.ppermute(part_b, 'ch', pairs).astype(jnp.float32)  3.55 us
    unnamed x10, local copies, waits for them, and re-layouts  3.14 us
  transfers between devices with their start and end apart: 4, of which 1 were waited for; matrix products, arithmetic and copies ran while one was open for 12% of the time, Pallas kernels for 33%

profile of v4, /device:TPU:16, one launch (start us, length us, event | category | flops | bytes accessed | tf_op | source)
XLA Modules:
  0.0 116.7 jit_solution(7440447802789944258)
XLA Ops:
  7.2 0.0 copy-start
  7.2 0.0 all-gather.2.cloned.1.call-start
  7.2 1.6 %pad_maximum_fusion.1 = bf16[64,1024]{1,0:T(8,128)(2,1)} fusion(bf16[64,512]{1,0:T(8,128)(2,1)} %param.25, bf16[64,512]{1,0:T(8,128)(2,1)} %param.24), kind=kLoop, calls=%fused_computation.14 | loop fusion | flops 262144 | bytes 262144 | tf_op jit(solution)/shard_map/concatenate | solution.py:323
  8.8 0.0 all-gather.2.cloned.1.call-update
  8.8 1.0 fusion.5
  9.9 0.7 collective-permute-start.1
  10.6 1.3 %collective-permute-start = (bf16[3,8192]{1,0:T(4,128)(2,1)S(1)}, bf16[3,8192]{1,0:T(4,128)(2,1)S(1)}, u32[]{:S(2)}, u32[]{:S(2)}) collective-permute-start(bf16[3,8192]{1,0:T(4,128)(2,1)S(1)} %get-tuple-element.13), channel_id=1, source_target_pairs={{1,2},{3,4},{5,6},{7,8},{9,10},{11,12},{13,14},{15,16},{17,18},{19... | collective-permute-start | bytes 147464 | tf_op jit(solution)/shard_map/ppermute | solution.py:24
  11.9 1.4 %fusion.6 = (f32[1,8192]{1,0:T(1,128)S(1)}, f32[1,8192]{1,0:T(1,128)S(1)}, f32[1,8192]{1,0:T(1,128)S(1)}, f32[1,8192]{1,0:T(1,128)S(1)}) fusion(f32[4,8192]{1,0:T(4,128)} %param.15), kind=kLoop, calls=%fused_computation.17 | loop fusion | bytes 262144 | tf_op jit(solution)/shard_map/slice | solution.py:343
  13.2 19.9 %swap_input.1 = bf16[2,32,8192]{2,1,0:T(8,128)(2,1)} custom-call(bf16[32,16384]{1,0:T(8,128)(2,1)} %src_ref.1), custom_call_target="tpu_custom_call" | custom-call | tf_op jit(solution)/shard_map/swap_input/pallas_call | solution.py:331
  33.1 0.0 copy-start.3
  33.2 0.0 collective-permute-done.1
  33.2 0.0 collective-permute-done
  33.2 1.5 %maximum_convert_fusion = f32[67,8192]{1,0:T(8,128)S(1)} fusion(bf16[64,8192]{1,0:T(8,128)(2,1)} %bitcast.12, bf16[3,8192]{1,0:T(4,128)(2,1)S(1)} %add.35), kind=kLoop, calls=%fused_computation.9 | loop fusion | flops 2195456 | bytes 3293184 | tf_op jit(solution)/shard_map/convert_element_type | solution.py:341
  34.7 0.0 copy-done.3
  34.7 1.3 %multiply_convert_fusion.act_ref = bf16[64,8192]{1,0:T(8,128)(2,1)S(1)} fusion(f32[67,8192]{1,0:T(8,128)S(1)} %maximum_convert_fusion, f32[8192]{0:T(1024)S(1)} %bitcast.16, f32[8192]{0:T(1024)S(1)} %bitcast.17, f32[8192]{0:T(1024)S(1)} %bitcast.15, f32[8192]{0:T(1024)S(1)} %bitcast.14, f32[8192]{0:T(1024)S(1)} %copy-done.3), kind=kLoop, calls=%fused_computation.8 | loop fusion | flops 6815744 | bytes 9601024 | tf_op jit(solution)/shard_map/convert_element_type | solution.py:345
  36.1 0.0 copy-done
  36.1 0.0 copy-start.1
  36.1 0.4 fusion.8
  36.6 5.1 %fusion.7 = f32[64,512]{1,0:T(8,128)S(1)} fusion(bf16[64,8192]{1,0:T(8,128)(2,1)S(1)} %multiply_convert_fusion.act_ref, bf16[8192,512]{1,0:T(8,128)(2,1)} %param.17), kind=kOutput, calls=%fused_computation.18 | convolution fusion | flops 536870912 | bytes 9568256 | tf_op jit(solution)/shard_map/dot_general | solution.py:346
  41.6 0.0 copy-done.1
  41.7 0.2 collective-permute-start.2
  41.9 0.8 dynamic-slice_multiply_fusion
  42.7 0.6 reshape.15.rate_ref
  43.3 3.6 %collective-permute-done.2 = bf16[64,544]{1,0:T(8,128)(2,1)S(1)} collective-permute-done((bf16[64,544]{1,0:T(8,128)(2,1)S(1)}, bf16[64,544]{1,0:T(8,128)(2,1)S(1)}, u32[]{:S(2)}, u32[]{:S(2)}) %collective-permute-start.2) | collective-permute-done | bytes 69664 | tf_op jit(solution)/shard_map/ppermute | solution.py:353
  46.8 0.6 slice.57.terms_ref
  47.4 0.6 slice.85.low_ref
  48.1 19.1 %first_pass.1 = (f32[8,512,128]{2,1,0:T(8,128)}, bf16[16,80,128]{2,1,0:T(8,128)(2,1)}, bf16[2,32,8192]{2,1,0:T(8,128)(2,1)}) custom-call(bf16[64,512]{1,0:T(8,128)(2,1)} %slice.85.low_ref, bf16[512,8192]{1,0:T(8,128)(2,1)} %up_ref.1, f32[1,8192]{1,0:T(1,128)} %bitcast.18, bf16[64,8192]{1,0:T(8,128)(2,1)} %copy-done.1, f32[64,32]{1,0:T(8,128)} %slice.57.terms_ref, ...), custom_call_target="tpu_custom_call" | custom-call | tf_op jit(solution)/shard_map/first_pass/pallas_call | solution.py:373
  67.2 0.0 all-gather.2.cloned.1.call-done.kv_ref
  67.2 22.1 %exchange.1 = (bf16[16,64,128]{2,1,0:T(8,128)(2,1)}, bf16[64,4096]{1,0:T(8,128)(2,1)}) custom-call(bf16[16,80,128]{2,1,0:T(8,128)(2,1)} %get-tuple-element.8.send_ref, f32[64,128]{1,0:T(8,128)} %reshape.15.rate_ref, bf16[64,4096]{1,0:T(8,128)(2,1)} %q_ref.1, bf16[1024,1024]{1,0:T(8,128)(2,1)} %all-gather.2.cloned.1.call-done.kv_ref), custom_call_target="tpu_custom_call" | custom-call | tf_op jit(solution)/shard_map/exchange/pallas_call | solution.py:400
  89.3 17.4 %second_pass.1 = bf16[32,16384]{1,0:T(8,128)(2,1)} custom-call(f32[8,512,128]{2,1,0:T(8,128)} %get-tuple-element.7.step_ref, bf16[64,8192]{1,0:T(8,128)(2,1)} %copy-done.1, f32[64,32]{1,0:T(8,128)} %slice.57.terms_ref, f32[16,8192]{1,0:T(8,128)} %decay_ref.3, bf16[16,64,128]{2,1,0:T(8,128)(2,1)} %get-tuple-element.9.incoming_ref, bf16[64,8192]{1,0:T(8,128)(2,1)} %bitcast.13, ...), custom_call_target="tpu_custom_call" | custom-call | tf_op jit(solution)/shard_map/second_pass/pallas_call | solution.py:417
  106.7 2.3 %copy.19 = bf16[32,16384]{1,0:T(8,128)(2,1)} copy(bf16[32,16384]{1,0:T(8,128)(2,1)} %second_pass.1) | data formatting | bytes 2097152
  109.1 0.8 copy.20
  (5 shorter events, 0.1 us)
Async XLA Ops:
  7.2 28.9 %copy-start = (bf16[8192,32]{0,1:T(8,128)(2,1)S(1)}, bf16[8192,32]{0,1:T(8,128)(2,1)}, u32[]{:S(2)}) copy-start(bf16[8192,32]{0,1:T(8,128)(2,1)} %param.18) | copy-start | bytes 1572868
  7.2 60.0 %all-gather.2.cloned.1.call-start = ((), (), s32[]{:S(2)}) async-start(), calls=%async_computation | async-start | bytes 2228224 | tf_op jit(solution)/shard_map/all_gather | solution.py:322
  9.9 23.3 %collective-permute-start.1 = (bf16[3,8192]{1,0:T(4,128)(2,1)S(1)}, bf16[3,8192]{1,0:T(4,128)(2,1)S(1)}, u32[]{:S(2)}, u32[]{:S(2)}) collective-permute-start(bf16[3,8192]{1,0:T(4,128)(2,1)S(1)} %get-tuple-element.12), channel_id=1, source_target_pairs={{1,3},{3,5},{5,7},{7,9},{9,11},{11,13},{13,15},{15,17},{17,19},{19... | collective-permute-start | bytes 147464 | tf_op jit(solution)/shard_map/ppermute | solution.py:24
  10.6 22.6 %collective-permute-start = (bf16[3,8192]{1,0:T(4,128)(2,1)S(1)}, bf16[3,8192]{1,0:T(4,128)(2,1)S(1)}, u32[]{:S(2)}, u32[]{:S(2)}) collective-permute-start(bf16[3,8192]{1,0:T(4,128)(2,1)S(1)} %get-tuple-element.13), channel_id=1, source_target_pairs={{1,2},{3,4},{5,6},{7,8},{9,10},{11,12},{13,14},{15,16},{17,18},{19... | collective-permute-start | bytes 147464 | tf_op jit(solution)/shard_map/ppermute | solution.py:24
  33.1 1.6 %copy-start.3 = (f32[8192]{0:T(1024)S(1)}, f32[8192]{0:T(1024)}, u32[]{:S(2)}) copy-start(f32[8192]{0:T(1024)} %param.16) | copy-start | bytes 98308
  36.1 5.5 %copy-start.1 = (bf16[64,8192]{1,0:T(8,128)(2,1)}, bf16[64,8192]{1,0:T(8,128)(2,1)S(1)}, u32[]{:S(2)}) copy-start(bf16[64,8192]{1,0:T(8,128)(2,1)S(1)} %multiply_convert_fusion.act_ref) | copy-start | bytes 3145732
  41.7 5.1 %collective-permute-start.2 = (bf16[64,544]{1,0:T(8,128)(2,1)S(1)}, bf16[64,544]{1,0:T(8,128)(2,1)S(1)}, u32[]{:S(2)}, u32[]{:S(2)}) collective-permute-start(bf16[64,544]{1,0:T(8,128)(2,1)S(1)} %fusion.4), channel_id=1, source_target_pairs={{0,1},{1,0},{2,3},{3,2},{4,5},{5,4},{6,7},{7,6},{8,9},{9,8},{10,11... | collective-permute-start | bytes 208904 | tf_op jit(solution)/shard_map/ppermute | solution.py:353
  106.7 2.3 %copy-start.2 = (bf16[64,4096]{1,0:T(8,128)(2,1)S(1)}, bf16[64,4096]{1,0:T(8,128)(2,1)}, u32[]{:S(2)}) copy-start(bf16[64,4096]{1,0:T(8,128)(2,1)} %get-tuple-element.21) | copy-start | bytes 1572868
Sparse Core Ops, SparseCore 0:
  10.7 40.5 all-gather.1

commit v5 on v4

--- a/solution.py
+++ b/solution.py
@@ -81,18 +81,9 @@
             pltpu.get_barrier_semaphore(), inc=1, device_id={axis: peer}, device_id_type=MESH)
 
 
-def first_pass(packing, n_ch, low_ref, up_ref, bias_ref, act_ref, terms_ref, decay_ref, gate_ref,
-               step_ref, packed_ref, gate_out, spread, act_rows, rates, pack,
-               keep_sem, send_sem, recv_sem):
+def first_pass(packing, low_ref, up_ref, bias_ref, act_ref, terms_ref, decay_ref,
+               step_ref, packed_ref, spread, act_rows, rates, pack):
     rows = act_ref.shape[0]
-    gates = swap_copies(n_ch, gate_ref, gate_out, keep_sem, send_sem, recv_sem)
-
-    @pl.when(pl.program_id(0) == 0)
-    def _():
-        greet("ch", n_ch)
-        pl.semaphore_wait(pltpu.get_barrier_semaphore(), n_ch - 1)
-        for copy in gates:
-            copy.start()
 
     @pl.when(pl.program_id(0) == 0)
     def _():
@@ -128,13 +119,8 @@
         pack[part, rows_state + subs : rows_state + 2 * subs] = (total - total_hi)[cut]
     packed_ref[...] = pack[...].astype(jnp.bfloat16)
 
-    @pl.when(pl.program_id(0) == pl.num_programs(0) - 1)
-    def _():
-        for copy in gates:
-            copy.wait()
-
-
-def second_pass(packing, n_ch, step_ref, act_ref, terms_ref, decay_ref, incoming_ref, gate_ref, skip_ref,
+
+def second_pass(packing, n_ch, step_ref, act_ref, terms_ref, decay_ref, incoming_ref, skip_ref,
                 out_ref, spread, act_rows, rates, outs, entering, wide, outbox,
                 keep_sem, send_sem, recv_sem):
     rows = act_ref.shape[0]
@@ -185,8 +171,6 @@
         cols = slice(sub * LANES, (sub + 1) * LANES)
         mixed = outs[pl.ds(sub, rows, stride=SUBS), :]
         mixed = mixed + skip_ref[:, cols] * act_ref[:, cols].astype(jnp.float32)
-        mixed = mixed.astype(jnp.bfloat16).astype(jnp.float32)
-        mixed = mixed * jax.nn.silu(gate_ref[:, cols].astype(jnp.float32))
         mixed = mixed.astype(jnp.bfloat16)
         at = pl.multiple_of(first + sub * LANES, LANES)
         for j in range(n_ch):
@@ -370,27 +354,25 @@
     rows_back = -(-rows_state // 16) * 16
     rows_all = -(-(rows_state + 2 * subs) // 16) * 16
     packing = (splits, subs, held, rows_state)
-    step_rows, packed, inner_gate = pl.pallas_call(
-        functools.partial(first_pass, packing, n_ch),
+    step_rows, packed = pl.pallas_call(
+        functools.partial(first_pass, packing),
         grid=(tiles,),
         in_specs=[whole((rows, rank)), cols(rank), cols(1), cols(rows), whole((rows, 2 * STATE)),
-                  cols(STATE), hbm],
-        out_specs=[step_spec, pl.BlockSpec((parts, rows_all, LANES), lambda i: (i, 0, 0)), hbm],
+                  cols(STATE)],
+        out_specs=[step_spec, pl.BlockSpec((parts, rows_all, LANES), lambda i: (i, 0, 0))],
         out_shape=[
             jax.ShapeDtypeStruct((tiles, tile_rows, LANES), f32),
             jax.ShapeDtypeStruct((n_ctx, rows_all, LANES), bf16),
-            swapped,
         ],
         scratch_shapes=[
             pltpu.VMEM((STATE * rows, LANES), f32),
             pltpu.VMEM((tile_rows, LANES), f32),
             pltpu.VMEM((STATE * SUBS, LANES), f32),
             pltpu.VMEM((parts, rows_all, LANES), f32),
-        ] + swap_sems,
-        compiler_params=pltpu.CompilerParams(
-            collective_id=3, has_side_effects=True, vmem_limit_bytes=limit),
+        ],
+        compiler_params=pltpu.CompilerParams(vmem_limit_bytes=limit),
         name="first_pass",
-    )(step_low, step_up, step_bias[None], activation, state_terms, decay_rate, mamba_gate)
+    )(step_low, step_up, step_bias[None], activation, state_terms, decay_rate)
 
     me = lax.axis_index("ctx")
     my_rate = lax.dynamic_slice(
@@ -414,13 +396,13 @@
         name="exchange",
     )(packed, my_rate, queries, kv)
 
-    mamba_out = pl.pallas_call(
+    scan_out = pl.pallas_call(
         functools.partial(second_pass, packing, n_ch),
         grid=(tiles,),
         in_specs=[
             step_spec, cols(rows), whole((rows, 2 * STATE)), cols(STATE),
             pl.BlockSpec((parts, rows_back, LANES), lambda i: (i, 0, 0)),
-            cols(rows), cols(1),
+            cols(1),
         ],
         out_specs=pl.BlockSpec(memory_space=pl.ANY),
         out_shape=jax.ShapeDtypeStruct(mamba_input.shape, bf16),
@@ -440,7 +422,8 @@
             collective_id=1, has_side_effects=True, vmem_limit_bytes=limit),
         name="second_pass",
     )(step_rows, activation, state_terms, decay_rate, incoming,
-      inner_gate.reshape(rows, channels), skip_gain[None])
+      skip_gain[None])
+    mamba_out = (scan_out.astype(f32) * jax.nn.silu(mamba_gate.astype(f32))).astype(bf16)
     return (mamba_out, attention_out)
 
 

time: 118 us -> 113 us (0.958)
  Pallas kernels: 78.5 us -> 73.7 us
  other arithmetic: 5.27 us -> 8.07 us
  local copies, waits for them, and re-layouts: 7.38 us -> 5.15 us
    pallas_call x1, Pallas kernels: 19.1 us -> 12.6 us  [local(): pl.pallas_call(functools.partial(first_pass, packing), grid=(tiles,), in_...]
    convert_element_type x0 -> x1, other arithmetic: none -> 2.84 us  [local(): (scan_out.astype(f32) * jax.nn.silu(mamba_gate.astype(f32))).astype(bf16)]
    unnamed x10 -> x11, local copies, waits for them, and re-layouts: 3.14 us -> 0.83 us
    pallas_call x1, Pallas kernels: 19.9 us -> 22.1 us  [local(): pl.pallas_call(functools.partial(swap_input, n_ch), in_specs=[hbm], out_s...]
  transfers between devices with their start and end apart: 4 -> 4, of which waited for: 1 -> 1; matrix products, arithmetic and copies ran while one was open for 12% -> 13% of each run, Pallas kernels for 33% -> 31%
where the time goes in v5:
time: 113 us; the launch traced here: 112 us
  Pallas kernels  73.7 us (65%)
  between operations  14.2 us (13%)
  other arithmetic  8.07 us (7%)
  matrix products  5.62 us (5%)
  local copies, waits for them, and re-layouts  5.15 us (5%)
  waiting for transfers between devices  3.07 us (3%)
  starting transfers between devices  2.07 us (2%)
    pallas_call x1, Pallas kernels, local(): pl.pallas_call(functools.partial(swap_input, n_ch), in_specs=[hbm], out_s...  22.1 us
    pallas_call x1, Pallas kernels, local(): pl.pallas_call(functools.partial(exchange, n_ctx, rows_state, subs), in_s...  21.6 us
    pallas_call x1, Pallas kernels, local(): pl.pallas_call(functools.partial(second_pass, packing, n_ch), grid=(tiles...  17.4 us
    pallas_call x1, Pallas kernels, local(): pl.pallas_call(functools.partial(first_pass, packing), grid=(tiles,), in_...  12.6 us
    dot_general x1, matrix products, local(): jnp.dot(activation, step_down, preferred_element_type=jnp.float32)  5.19 us
    ppermute x1, waiting for transfers between devices, local(): summed = summed + lax.ppermute(part_b, 'ch', pairs).astype(jnp.float32)  3.04 us
    convert_element_type x1, other arithmetic, local(): (scan_out.astype(f32) * jax.nn.silu(mamba_gate.astype(f32))).astype(bf16)  2.84 us
  transfers between devices with their start and end apart: 4, of which 1 were waited for; matrix products, arithmetic and copies ran while one was open for 13% of the time, Pallas kernels for 31%

profile of v5, /device:TPU:16, one launch (start us, length us, event | category | flops | bytes accessed | tf_op | source)
XLA Modules:
  0.0 111.9 jit_solution(4239643812361557001)
XLA Ops:
  7.2 0.0 copy-start
  7.2 0.0 all-gather.2.cloned.1.call-start
  7.2 1.1 fusion.10
  8.3 1.3 %collective-permute-start = (bf16[3,8192]{1,0:T(4,128)(2,1)S(1)}, bf16[3,8192]{1,0:T(4,128)(2,1)S(1)}, u32[]{:S(2)}, u32[]{:S(2)}) collective-permute-start(bf16[3,8192]{1,0:T(4,128)(2,1)S(1)} %get-tuple-element.11), channel_id=1, source_target_pairs={{1,2},{3,4},{5,6},{7,8},{9,10},{11,12},{13,14},{15,16},{17,18},{19... | collective-permute-start | bytes 147464 | tf_op jit(solution)/shard_map/ppermute | solution.py:24
  9.6 0.7 collective-permute-start.1
  10.3 1.5 %pad_maximum_fusion.1 = bf16[64,1024]{1,0:T(8,128)(2,1)} fusion(bf16[64,512]{1,0:T(8,128)(2,1)} %param.25, bf16[64,512]{1,0:T(8,128)(2,1)} %param.24), kind=kLoop, calls=%fused_computation.21 | loop fusion | flops 262144 | bytes 262144 | tf_op jit(solution)/shard_map/concatenate | solution.py:307
  11.8 0.0 all-gather.2.cloned.1.call-update
  11.9 1.4 %fusion.11 = (f32[1,8192]{1,0:T(1,128)S(1)}, f32[1,8192]{1,0:T(1,128)S(1)}, f32[1,8192]{1,0:T(1,128)S(1)}, f32[1,8192]{1,0:T(1,128)S(1)}) fusion(f32[4,8192]{1,0:T(4,128)} %param.15), kind=kLoop, calls=%fused_computation.24 | loop fusion | bytes 262144 | tf_op jit(solution)/shard_map/slice | solution.py:327
  13.2 22.1 %swap_input.1 = bf16[2,32,8192]{2,1,0:T(8,128)(2,1)} custom-call(bf16[32,16384]{1,0:T(8,128)(2,1)} %src_ref.1), custom_call_target="tpu_custom_call" | custom-call | tf_op jit(solution)/shard_map/swap_input/pallas_call | solution.py:315
  35.4 0.0 copy-start.4
  35.4 0.0 collective-permute-done
  35.4 0.0 collective-permute-done.1
  35.4 1.5 %maximum_convert_fusion = f32[67,8192]{1,0:T(8,128)S(1)} fusion(bf16[64,8192]{1,0:T(8,128)(2,1)} %bitcast.11, bf16[3,8192]{1,0:T(4,128)(2,1)S(1)} %add.39), kind=kLoop, calls=%fused_computation.16 | loop fusion | flops 2195456 | bytes 3293184 | tf_op jit(solution)/shard_map/convert_element_type | solution.py:325
  37.0 0.0 copy-done.4
  37.0 1.3 %multiply_convert_fusion.act_ref = bf16[64,8192]{1,0:T(8,128)(2,1)S(1)} fusion(f32[67,8192]{1,0:T(8,128)S(1)} %maximum_convert_fusion, f32[8192]{0:T(1024)S(1)} %bitcast.14, f32[8192]{0:T(1024)S(1)} %bitcast.15, f32[8192]{0:T(1024)S(1)} %bitcast.13, f32[8192]{0:T(1024)S(1)} %bitcast.12, f32[8192]{0:T(1024)S(1)} %copy-done.4), kind=kLoop, calls=%fused_computation.14 | loop fusion | flops 6815744 | bytes 9601024 | tf_op jit(solution)/shard_map/convert_element_type | solution.py:329
  38.3 0.0 copy-done
  38.3 0.0 copy-start.1
  38.3 0.4 fusion.13
  38.8 5.2 %fusion.12 = f32[64,512]{1,0:T(8,128)S(1)} fusion(bf16[64,8192]{1,0:T(8,128)(2,1)S(1)} %multiply_convert_fusion.act_ref, bf16[8192,512]{1,0:T(8,128)(2,1)} %param.17), kind=kOutput, calls=%fused_computation.25 | convolution fusion | flops 536870912 | bytes 9568256 | tf_op jit(solution)/shard_map/dot_general | solution.py:330
  44.0 0.1 collective-permute-start.2
  44.1 0.8 dynamic-slice_multiply_fusion
  44.9 0.6 reshape.12.rate_ref
  45.5 3.0 %collective-permute-done.2 = bf16[64,544]{1,0:T(8,128)(2,1)S(1)} collective-permute-done((bf16[64,544]{1,0:T(8,128)(2,1)S(1)}, bf16[64,544]{1,0:T(8,128)(2,1)S(1)}, u32[]{:S(2)}, u32[]{:S(2)}) %collective-permute-start.2) | collective-permute-done | bytes 69664 | tf_op jit(solution)/shard_map/ppermute | solution.py:337
  48.5 0.6 slice.85.low_ref
  49.2 0.6 slice.57.terms_ref
  49.8 12.6 %first_pass.1 = (f32[8,512,128]{2,1,0:T(8,128)}, bf16[16,80,128]{2,1,0:T(8,128)(2,1)}) custom-call(bf16[64,512]{1,0:T(8,128)(2,1)} %slice.85.low_ref, bf16[512,8192]{1,0:T(8,128)(2,1)} %up_ref.1, f32[1,8192]{1,0:T(1,128)} %bitcast.16, bf16[64,8192]{1,0:T(8,128)(2,1)} %copy-done.1, f32[64,32]{1,0:T(8,128)} %slice.57.terms_ref, f32[16,8192]{1,0:T(8,128)} %decay_ref.3), custom_call_target="tpu_custom_call" | custom-call | tf_op jit(solution)/shard_map/first_pass/pallas_call | solution.py:357
  62.4 0.0 all-gather.2.cloned.1.call-done.kv_ref
  62.4 21.6 %exchange.1 = (bf16[16,64,128]{2,1,0:T(8,128)(2,1)}, bf16[64,4096]{1,0:T(8,128)(2,1)}) custom-call(bf16[16,80,128]{2,1,0:T(8,128)(2,1)} %get-tuple-element.7.send_ref, f32[64,128]{1,0:T(8,128)} %reshape.12.rate_ref, bf16[64,4096]{1,0:T(8,128)(2,1)} %q_ref.1, bf16[1024,1024]{1,0:T(8,128)(2,1)} %all-gather.2.cloned.1.call-done.kv_ref), custom_call_target="tpu_custom_call" | custom-call | tf_op jit(solution)/shard_map/exchange/pallas_call | solution.py:382
  84.0 0.0 copy-start.2
  84.0 17.4 %second_pass.1 = bf16[32,16384]{1,0:T(8,128)(2,1)} custom-call(f32[8,512,128]{2,1,0:T(8,128)} %get-tuple-element.6.step_ref, bf16[64,8192]{1,0:T(8,128)(2,1)} %copy-done.1, f32[64,32]{1,0:T(8,128)} %slice.57.terms_ref, f32[16,8192]{1,0:T(8,128)} %decay_ref.3, bf16[16,64,128]{2,1,0:T(8,128)(2,1)} %get-tuple-element.8.incoming_ref, f32[1,8192]{1,0:T(1,128)} %bitcast.17), custom_call_target="tpu_custom_call" | custom-call | tf_op jit(solution)/shard_map/second_pass/pallas_call | solution.py:399
  101.5 2.8 %fusion.8 = bf16[32,16384]{1,0:T(8,128)(2,1)} fusion(bf16[32,16384]{1,0:T(8,128)(2,1)S(1)} %copy-done.2, bf16[32,16384]{1,0:T(8,128)(2,1)} %second_pass.1), kind=kLoop, calls=%fused_computation.15 | loop fusion | flops 4194304 | bytes 3145728 | tf_op jit(solution)/shard_map/convert_element_type | solution.py:426
  104.3 0.8 copy.18
  (7 shorter events, 0.1 us)
Async XLA Ops:
  7.2 31.2 %copy-start = (bf16[8192,32]{0,1:T(8,128)(2,1)S(1)}, bf16[8192,32]{0,1:T(8,128)(2,1)}, u32[]{:S(2)}) copy-start(bf16[8192,32]{0,1:T(8,128)(2,1)} %param.18) | copy-start | bytes 1572868
  7.2 55.2 %all-gather.2.cloned.1.call-start = ((), (), s32[]{:S(2)}) async-start(), calls=%async_computation | async-start | bytes 2228224 | tf_op jit(solution)/shard_map/all_gather | solution.py:306
  8.3 27.1 %collective-permute-start = (bf16[3,8192]{1,0:T(4,128)(2,1)S(1)}, bf16[3,8192]{1,0:T(4,128)(2,1)S(1)}, u32[]{:S(2)}, u32[]{:S(2)}) collective-permute-start(bf16[3,8192]{1,0:T(4,128)(2,1)S(1)} %get-tuple-element.11), channel_id=1, source_target_pairs={{1,2},{3,4},{5,6},{7,8},{9,10},{11,12},{13,14},{15,16},{17,18},{19... | collective-permute-start | bytes 147464 | tf_op jit(solution)/shard_map/ppermute | solution.py:24
  9.6 25.8 %collective-permute-start.1 = (bf16[3,8192]{1,0:T(4,128)(2,1)S(1)}, bf16[3,8192]{1,0:T(4,128)(2,1)S(1)}, u32[]{:S(2)}, u32[]{:S(2)}) collective-permute-start(bf16[3,8192]{1,0:T(4,128)(2,1)S(1)} %get-tuple-element.10), channel_id=1, source_target_pairs={{1,3},{3,5},{5,7},{7,9},{9,11},{11,13},{13,15},{15,17},{17,19},{19... | collective-permute-start | bytes 147464 | tf_op jit(solution)/shard_map/ppermute | solution.py:24
  35.4 1.6 %copy-start.4 = (f32[8192]{0:T(1024)S(1)}, f32[8192]{0:T(1024)}, u32[]{:S(2)}) copy-start(f32[8192]{0:T(1024)} %param.16) | copy-start | bytes 98308
  38.3 5.7 %copy-start.1 = (bf16[64,8192]{1,0:T(8,128)(2,1)}, bf16[64,8192]{1,0:T(8,128)(2,1)S(1)}, u32[]{:S(2)}) copy-start(bf16[64,8192]{1,0:T(8,128)(2,1)S(1)} %multiply_convert_fusion.act_ref) | copy-start | bytes 3145732
  44.0 4.5 %collective-permute-start.2 = (bf16[64,544]{1,0:T(8,128)(2,1)S(1)}, bf16[64,544]{1,0:T(8,128)(2,1)S(1)}, u32[]{:S(2)}, u32[]{:S(2)}) collective-permute-start(bf16[64,544]{1,0:T(8,128)(2,1)S(1)} %fusion.9), channel_id=1, source_target_pairs={{0,1},{1,0},{2,3},{3,2},{4,5},{5,4},{6,7},{7,6},{8,9},{9,8},{10,11... | collective-permute-start | bytes 208904 | tf_op jit(solution)/shard_map/ppermute | solution.py:337
  84.0 17.4 %copy-start.2 = (bf16[32,16384]{1,0:T(8,128)(2,1)S(1)}, bf16[32,16384]{1,0:T(8,128)(2,1)}, u32[]{:S(2)}) copy-start(bf16[32,16384]{1,0:T(8,128)(2,1)} %param.14) | copy-start | bytes 3145732
  101.5 2.9 %copy-start.3 = (bf16[64,4096]{1,0:T(8,128)(2,1)S(1)}, bf16[64,4096]{1,0:T(8,128)(2,1)}, u32[]{:S(2)}) copy-start(bf16[64,4096]{1,0:T(8,128)(2,1)} %get-tuple-element.19) | copy-start | bytes 1572868
Sparse Core Ops, SparseCore 0:
  12.0 43.1 all-gather.1
